TPU v7x, 32 devices: a whole 2x2x4 slice. The times are simulated.
32 devices in a mesh: pole: 2 (over x), row: 16 (over z, y, core).
Axes of the slice: x: 2, y: 2, z: 4, core: 2. Of those that a mesh axis runs over, the one named last changes fastest.
Arguments:
- inverse_root: bfloat16 [8192, 4096], P(('pole', 'row')), parts along dimension 0
- lower_panel: bfloat16 [8192, 512], P(('pole', 'row')), parts along dimension 0, may hold values from -0.3984375 to 0.3984375
- coupling: int32 [16], replicated, may hold values from 0 to 2
- child_inverse: float32 [1024, 256], P(('pole', 'row')), parts along dimension 0, may hold values from -3 to 3
Outputs:
- offdiag: float32 [8192, 512], P(('pole', 'row')), parts along dimension 0
- child_diag: float32 [1024, 256], P(('pole', 'row')), parts along dimension 0
There are 2 independent parts, one for each index of `pole`. A program takes and returns all parts, laid end to end along the dimension named above; an argument that names none is the same for every part. Nothing has to cross between parts.
Inputs may be any that keep to these rules, and one draw needn't show every extreme that they name: `coupling`: entry t names the child supernode coupled to tile row t of the separator; the value 2 means that the tile row couples to no child.
All inputs are finite; a program needn't handle non-finite values.
Results may differ from a plain program's by a relative error of at most 0.0003.
Values may be sent and summed in bfloat16 or wider, within the bound.
No kernel may reach another device: no remote copies, remote signals or barrier semaphores. Data moves between devices by JAX's collectives and lax.ppermute only.
A program may use at most 64 MiB of HBM per device.

v0:
```python
import jax
import jax.numpy as jnp
from jax import lax
from jax.sharding import PartitionSpec as P

NCH = 2
CW = 256


def per_device(inverse_root, lower_panel, coupling, child_inverse):
    rows = inverse_root.shape[0]
    width = lower_panel.shape[1]
    place = lax.axis_index("row")
    own_child = coupling[place]
    col_child = jnp.arange(width) // CW
    own_mask = own_child == col_child
    panel = jnp.where(own_mask[None, :], lower_panel, jnp.zeros_like(lower_panel))
    product = jnp.dot(
        inverse_root,
        lax.all_gather(panel, "row", axis=0, tiled=True),
        preferred_element_type=jnp.float32,
    )
    offdiag = jnp.where(own_mask[None, :], -product, jnp.float32(0.0))
    left = panel.astype(jnp.float32).reshape(rows, NCH, CW)
    right = offdiag.reshape(rows, NCH, CW)
    term = jnp.einsum(
        "rkc,rkd->kcd",
        left,
        right,
        precision=lax.Precision.HIGHEST,
        preferred_element_type=jnp.float32,
    )
    term = term.reshape(NCH * CW, CW)
    shares = lax.psum_scatter(term, "row", scatter_dimension=0, tiled=True)
    child_diag = child_inverse - shares
    return (offdiag, child_diag)


def solution(mesh):
    in_specs = (P(("pole", "row"), None), P(("pole", "row"), None), P(), P(("pole", "row"), None))
    out_specs = (P(("pole", "row"), None), P(("pole", "row"), None))
    return jax.shard_map(
        per_device, mesh=mesh, in_specs=in_specs, out_specs=out_specs, check_vma=False
    )
```

profile of v0, /device:TPU:0, one launch (start us, length us, event | category | flops | bytes accessed | tf_op | source)
XLA Modules:
  0.0 131.8 jit_solution(17916634841388460774)
XLA Ops:
  7.2 0.0 copy-start
  7.2 0.0 all-gather.2.cloned.1.call-start
  7.2 1.4 %dynamic_slice.3 = s32[1]{0:T(128)} dynamic-slice(s32[16]{0:T(128)} %param.6, s32[]{:T(128)S(6)} %select_n.23), dynamic_slice_sizes={1} | dynamic-slice | bytes 12 | tf_op jit(solution)/shard_map/dynamic_slice | solution.py:14
  8.6 0.7 fusion.1
  9.3 1.7 %broadcast_select_fusion = bf16[256,512]{1,0:T(8,128)(2,1)} fusion(bf16[256,512]{1,0:T(8,128)(2,1)} %param.5, pred[512]{0:T(512)(128)(4,1)S(1)} %fusion.1), kind=kLoop, calls=%fused_computation.2 | loop fusion | flops 131072 | bytes 524800 | tf_op jit(solution)/shard_map/jit(_where)/select_n | solution.py:17
  10.9 0.0 all-gather.2.cloned.1.call-update
  11.0 0.0 reduce-scatter.2.cloned.1.call-start
  11.0 1.1 copy.10
  12.1 0.0 copy-start.1
  12.1 52.3 %all-gather.2.cloned.1.call-done = bf16[4096,512]{1,0:T(8,128)(2,1)} async-done(((bf16[256,512]{1,0:T(8,128)(2,1)}), bf16[4096,512]{1,0:T(8,128)(2,1)}) %all-gather.2.cloned.1.call-update) | async-done | bytes 4194320 | tf_op jit(solution)/shard_map/all_gather | solution.py:20
  64.4 0.0 copy-done
  64.4 3.5 %fusion = f32[512,256]{1,0:T(8,128)S(1)} fusion(bf16[4096,512]{1,0:T(8,128)(2,1)} %all-gather.2.cloned.1.call-done, bf16[256,4096]{1,0:T(8,128)(2,1)S(1)} %copy-done, pred[512]{0:T(512)(128)(4,1)S(1)} %fusion.1), kind=kOutput, calls=%fused_computation.1 | convolution fusion | flops 1074003968 | bytes 6816256 | tf_op jit(solution)/shard_map/dot_general | solution.py:18
  67.9 1.2 fusion.5
  69.1 0.0 reduce-scatter.2.cloned.1.call-update
  69.1 1.0 copy.8
  70.1 53.4 %reduce-scatter.2.cloned.1.call-done = f32[32,256]{1,0:T(8,128)} async-done(((f32[512,256]{1,0:T(8,128)}), f32[32,256]{1,0:T(8,128)}) %reduce-scatter.2.cloned.1.call-update) | async-done | bytes 32784 | tf_op jit(solution)/shard_map/reduce_scatter | solution.py:34
  123.5 0.0 copy-done.1
  123.5 1.4 %sub.10 = f32[32,256]{1,0:T(8,128)} subtract(f32[32,256]{1,0:T(8,128)S(1)} %copy-done.1, f32[32,256]{1,0:T(8,128)} %reduce-scatter.2.cloned.1.call-done) | non-fusion elementwise | flops 8192 | bytes 98304 | tf_op jit(solution)/shard_map/sub | solution.py:35
Async XLA Ops:
  7.2 57.2 %copy-start = (bf16[256,4096]{1,0:T(8,128)(2,1)S(1)}, bf16[256,4096]{1,0:T(8,128)(2,1)}, u32[]{:S(2)}) copy-start(bf16[256,4096]{1,0:T(8,128)(2,1)} %param.4) | copy-start | bytes 6291460
  7.2 57.2 %all-gather.2.cloned.1.call-start = ((), (), s32[]{:S(2)}) async-start(), calls=%async_computation.1 | async-start | bytes 4456448 | tf_op jit(solution)/shard_map/all_gather | solution.py:20
  11.0 112.6 %reduce-scatter.2.cloned.1.call-start = ((), (), s32[]{:S(2)}) async-start(), calls=%async_computation.2 | async-start | bytes 557056 | tf_op jit(solution)/shard_map/reduce_scatter | solution.py:34
  12.1 111.4 %copy-start.1 = (f32[32,256]{1,0:T(8,128)S(1)}, f32[32,256]{1,0:T(8,128)}, u32[]{:S(2)}) copy-start(f32[32,256]{1,0:T(8,128)} %param.7) | copy-start | bytes 98308
Sparse Core Ops, SparseCore 0:
  11.1 53.2 all-gather.1
  69.3 54.2 reduce-scatter.1
where the time goes:
time: 132 us
  waiting for transfers between devices  106 us (80%)
  between operations  14.1 us (11%)
  matrix products  4.72 us (4%)
  other arithmetic  3.7 us (3%)
  local copies, waits for them, and re-layouts  3.47 us (3%)
    reduce_scatter x1, waiting for transfers between devices, per_device(): shares = lax.psum_scatter(term, 'row', scatter_dimension=0, tiled=True)  53.4 us
    all_gather x1, waiting for transfers between devices, per_device(): lax.all_gather(panel, 'row', axis=0, tiled=True)  52.3 us
    dot_general x1, matrix products, per_device(): jnp.dot(inverse_root, lax.all_gather(panel, 'row', axis=0, tiled=True), p...  3.49 us
  transfers between devices with their start and end apart: 2, of which 2 were waited for; matrix products, arithmetic and copies ran while one was open for 2% of the time, Pallas kernels for 0%

commit v1 on v0

v1 whole, which is shorter than its diff:
```python
import functools

import jax
import jax.numpy as jnp
from jax import lax
from jax.experimental import pallas as pl
from jax.experimental.pallas import tpu as pltpu
from jax.sharding import PartitionSpec as P

NCH = 2
CW = 256


def exchange(block, n, mask):
    return lax.ppermute(block, "row", [(i, i ^ mask) for i in range(n)])


def compact_kernel(coupling_ref, panel_ref, block_ref):
    child = coupling_ref[lax.axis_index("row")]
    start = pl.multiple_of(jnp.minimum(child, NCH - 1) * CW, CW)
    block_ref[...] = panel_ref[:, pl.ds(start, CW)]


def product_kernel(n, coupling_ref, inverse_ref, *refs):
    block_refs = refs[:n]
    offdiag_ref, send_ref, keep_ref, total = refs[n:]
    rows = inverse_ref.shape[0]
    me = lax.axis_index("row")
    child = coupling_ref[me]
    total[...] = jnp.zeros_like(total)
    for offset in range(n):
        tile = me ^ offset

        @pl.when((coupling_ref[tile] == child) & (child < NCH))
        def _():
            start = pl.multiple_of(tile * rows, rows)
            total[...] += jnp.dot(
                inverse_ref[:, pl.ds(start, rows)],
                block_refs[offset][...],
                preferred_element_type=jnp.float32,
            )

    product = total[...]
    zero = jnp.zeros_like(product)
    for k in range(NCH):
        offdiag_ref[:, k * CW:(k + 1) * CW] = jnp.where(child == k, -product, zero)
    left = block_refs[0][...]
    term = zero
    rest = product
    for _ in range(3):
        part = rest.astype(jnp.bfloat16)
        rest = rest - part.astype(jnp.float32)
        term += lax.dot_general(
            left, part, (((0,), (0,)), ((), ())), preferred_element_type=jnp.float32
        )
    piece = NCH * CW // n
    core = lax.rem(me, 2)
    for q in range(CW // piece // 2):
        low = term[2 * q * piece:(2 * q + 1) * piece]
        high = term[(2 * q + 1) * piece:(2 * q + 2) * piece]
        keep_ref[q * piece:(q + 1) * piece] = jnp.where(core == 0, low, high)
        send_ref[q * piece:(q + 1) * piece] = jnp.where(core == 0, high, low)


def pieces_kernel(n, coupling_ref, keep_ref, got_ref, *out_refs):
    piece = NCH * CW // n
    per_child = n // NCH // 2
    me = lax.axis_index("row")
    mine = coupling_ref[me]
    other = coupling_ref[me ^ 1]
    for offset in range(n // 2):
        place = lax.div(me ^ (2 * offset), 2)
        child = lax.div(place, per_child)
        start = pl.multiple_of(lax.rem(place, per_child) * piece, piece)
        kept = keep_ref[pl.ds(start, piece)]
        got = got_ref[pl.ds(start, piece)]
        zero = jnp.zeros_like(kept)
        out_refs[offset][...] = jnp.where(mine == child, kept, zero) + jnp.where(
            other == child, got, zero
        )


def per_device(n, inverse_root, lower_panel, coupling, child_inverse):
    rows = inverse_root.shape[0]
    smem = pl.BlockSpec(memory_space=pltpu.SMEM)
    vmem = pl.BlockSpec(memory_space=pltpu.VMEM)
    block = pl.pallas_call(
        compact_kernel,
        out_shape=jax.ShapeDtypeStruct((rows, CW), lower_panel.dtype),
        in_specs=[smem, vmem],
        out_specs=vmem,
        name="compact",
    )(coupling, lower_panel)
    held = {0: block}
    for offset in sorted(range(1, n), key=lambda o: (o.bit_count(), -o)):
        mask = offset & -offset
        held[offset] = exchange(held[offset ^ mask], n, mask)
    offdiag, send, keep = pl.pallas_call(
        functools.partial(product_kernel, n),
        out_shape=[
            jax.ShapeDtypeStruct((rows, NCH * CW), jnp.float32),
            jax.ShapeDtypeStruct((CW // 2, CW), jnp.float32),
            jax.ShapeDtypeStruct((CW // 2, CW), jnp.float32),
        ],
        in_specs=[smem] + [vmem] * (n + 1),
        out_specs=[vmem] * 3,
        scratch_shapes=[pltpu.VMEM((rows, CW), jnp.float32)],
        compiler_params=pltpu.CompilerParams(vmem_limit_bytes=48 * 2**20),
        name="product",
    )(coupling, inverse_root, *[held[offset] for offset in range(n)])
    got = exchange(send, n, 1)
    piece = NCH * CW // n
    parts = pl.pallas_call(
        functools.partial(pieces_kernel, n),
        out_shape=[jax.ShapeDtypeStruct((piece, CW), jnp.float32)] * (n // 2),
        in_specs=[smem, vmem, vmem],
        out_specs=[vmem] * (n // 2),
        name="pieces",
    )(coupling, keep, got)
    child_diag = child_inverse + parts[0]
    for offset in range(1, n // 2):
        child_diag = child_diag + exchange(parts[offset], n, 2 * offset)
    return offdiag, child_diag


def solution(mesh):
    split = P(("pole", "row"), None)
    return jax.shard_map(
        functools.partial(per_device, mesh.shape["row"]),
        mesh=mesh,
        in_specs=(split, split, P(), split),
        out_specs=(split, split),
        check_vma=False,
    )
```

time: 132 us -> 54.9 us (0.42)
  waiting for transfers between devices: 106 us -> 17.4 us
  starting transfers between devices: 0.08 us -> 25.9 us
  between operations: 14.1 us -> 0.69 us
  Pallas kernels: 0 us -> 4.93 us
  matrix products: 4.72 us -> 0 us
  other arithmetic: 3.7 us -> 1.39 us
    reduce_scatter x1 -> x0, waiting for transfers between devices: 53.4 us -> none  [per_device(): shares = lax.psum_scatter(term, 'row', scatter_dimension=0, tiled=True)]
    all_gather x1 -> x0, waiting for transfers between devices: 52.3 us -> none  [per_device(): lax.all_gather(panel, 'row', axis=0, tiled=True)]
    ppermute x0 -> x23, starting transfers between devices: none -> 25.9 us  [exchange(): return lax.ppermute(block, 'row', [(i, i ^ mask) for i in range(n)])]
    ppermute x0 -> x23, waiting for transfers between devices: none -> 17.4 us  [exchange(): return lax.ppermute(block, 'row', [(i, i ^ mask) for i in range(n)])]
    pallas_call x0 -> x3, Pallas kernels: none -> 4.93 us  [the longest x1 1.73 us: per_device(): pl.pallas_call(functools.partial(pieces_kernel, n), out_shape=[jax.ShapeD...]
    dot_general x2 -> x0, matrix products: 4.72 us -> none  [the longest x1 3.49 us: per_device(): jnp.dot(inverse_root, lax.all_gather(panel, 'row', axis=0, tiled=True), p...]
    unnamed x5 -> x12, local copies, waits for them, and re-layouts: 1.01 us -> 4.45 us
    select_n x1 -> x0, other arithmetic: 1.68 us -> none  [per_device(): jnp.where(own_mask[None, :], lower_panel, jnp.zeros_like(lower_panel))]
  transfers between devices with their start and end apart: 2 -> 23, of which waited for: 2 -> 9; matrix products, arithmetic and copies ran while one was open for 2% -> 0% of each run, Pallas kernels for 0% -> 0%
where the time goes in v1:
time: 54.9 us; the launch traced here: 54.8 us
  starting transfers between devices  25.9 us (47%)
  waiting for transfers between devices  17.4 us (32%)
  Pallas kernels  4.93 us (9%)
  local copies, waits for them, and re-layouts  4.45 us (8%)
  other arithmetic  1.39 us (3%)
  between operations  0.69 us (1%)
    ppermute x23, starting transfers between devices, exchange(): return lax.ppermute(block, 'row', [(i, i ^ mask) for i in range(n)])  25.9 us
    ppermute x23, waiting for transfers between devices, exchange(): return lax.ppermute(block, 'row', [(i, i ^ mask) for i in range(n)])  17.4 us
    unnamed x12, local copies, waits for them, and re-layouts  4.45 us
    pallas_call x1, Pallas kernels, per_device(): pl.pallas_call(functools.partial(pieces_kernel, n), out_shape=[jax.ShapeD...  1.73 us
    pallas_call x1, Pallas kernels, per_device(): pl.pallas_call(compact_kernel, out_shape=jax.ShapeDtypeStruct((rows, CW),...  1.64 us
    pallas_call x1, Pallas kernels, per_device(): pl.pallas_call(functools.partial(product_kernel, n), out_shape=[jax.Shape...  1.56 us
    add x1, other arithmetic, per_device(): child_diag = child_diag + exchange(parts[offset], n, 2 * offset)  1.39 us
  transfers between devices with their start and end apart: 23, of which 9 were waited for; matrix products, arithmetic and copies ran while one was open for 0% of the time, Pallas kernels for 0%

profile of v1, /device:TPU:0, one launch (start us, length us, event | category | flops | bytes accessed | tf_op | source)
XLA Modules:
  0.0 54.8 jit_solution(2839481575627597009)
XLA Ops:
  0.6 1.6 %compact.1.refs_0_ = bf16[256,256]{1,0:T(8,128)(2,1)} custom-call(s32[16]{0:T(128)} %coupling_ref.5, bf16[256,512]{1,0:T(8,128)(2,1)} %panel_ref.1), custom_call_target="tpu_custom_call" | custom-call | tf_op jit(solution)/shard_map/compact/pallas_call | solution.py:87
  2.3 4.0 %collective-permute-start.7 = (bf16[256,256]{1,0:T(8,128)(2,1)}, bf16[256,256]{1,0:T(8,128)(2,1)S(1)}, u32[]{:S(2)}, u32[]{:S(2)}) collective-permute-start(bf16[256,256]{1,0:T(8,128)(2,1)} %compact.1.refs_0_), channel_id=1, source_target_pairs={{0,8},{1,9},{2,10},{3,11},{4,12},{5,13},{6,14},{7,15},{8,0},{9,1},... | collective-permute-start | bytes 393224 | tf_op jit(solution)/shard_map/ppermute | solution.py:15
  6.3 1.6 %collective-permute-start.3 = (bf16[256,256]{1,0:T(8,128)(2,1)}, bf16[256,256]{1,0:T(8,128)(2,1)S(1)}, u32[]{:S(2)}, u32[]{:S(2)}) collective-permute-start(bf16[256,256]{1,0:T(8,128)(2,1)} %compact.1.refs_0_), channel_id=1, source_target_pairs={{0,4},{1,5},{2,6},{3,7},{4,0},{5,1},{6,2},{7,3},{8,12},{9,13},{10,... | collective-permute-start | bytes 393224 | tf_op jit(solution)/shard_map/ppermute | solution.py:15
  7.9 1.5 %collective-permute-start.1 = (bf16[256,256]{1,0:T(8,128)(2,1)}, bf16[256,256]{1,0:T(8,128)(2,1)S(1)}, u32[]{:S(2)}, u32[]{:S(2)}) collective-permute-start(bf16[256,256]{1,0:T(8,128)(2,1)} %compact.1.refs_0_), channel_id=1, source_target_pairs={{0,2},{1,3},{2,0},{3,1},{4,6},{5,7},{6,4},{7,5},{8,10},{9,11},{10,... | collective-permute-start | bytes 393224 | tf_op jit(solution)/shard_map/ppermute | solution.py:15
  9.4 0.0 collective-permute-start
  9.4 3.5 %collective-permute-done.7.refs_8_ = bf16[256,256]{1,0:T(8,128)(2,1)S(1)} collective-permute-done((bf16[256,256]{1,0:T(8,128)(2,1)}, bf16[256,256]{1,0:T(8,128)(2,1)S(1)}, u32[]{:S(2)}, u32[]{:S(2)}) %collective-permute-start.7) | collective-permute-done | bytes 131104 | tf_op jit(solution)/shard_map/ppermute | solution.py:15
  12.9 0.7 %collective-permute-start.11 = (bf16[256,256]{1,0:T(8,128)(2,1)S(1)}, bf16[256,256]{1,0:T(8,128)(2,1)S(1)}, u32[]{:S(2)}, u32[]{:S(2)}) collective-permute-start(bf16[256,256]{1,0:T(8,128)(2,1)S(1)} %collective-permute-done.7.refs_8_), channel_id=1, source_target_pairs={{0,4},{1,5},{2,6},{3,7},{4,0},{5,1},{6,2},{7,3},{8,12},{9,13},{10,... | collective-permute-start | bytes 393224 | tf_op jit(solution)/shard_map/ppermute | solution.py:15
  13.7 1.5 %collective-permute-start.9 = (bf16[256,256]{1,0:T(8,128)(2,1)S(1)}, bf16[256,256]{1,0:T(8,128)(2,1)S(1)}, u32[]{:S(2)}, u32[]{:S(2)}) collective-permute-start(bf16[256,256]{1,0:T(8,128)(2,1)S(1)} %collective-permute-done.7.refs_8_), channel_id=1, source_target_pairs={{0,2},{1,3},{2,0},{3,1},{4,6},{5,7},{6,4},{7,5},{8,10},{9,11},{10,... | collective-permute-start | bytes 393224 | tf_op jit(solution)/shard_map/ppermute | solution.py:15
  15.2 0.0 collective-permute-done.3.refs_4_
  15.2 0.0 collective-permute-start.8
  15.2 0.0 collective-permute-done.1.refs_2_
  15.2 0.6 %collective-permute-start.5 = (bf16[256,256]{1,0:T(8,128)(2,1)S(1)}, bf16[256,256]{1,0:T(8,128)(2,1)S(1)}, u32[]{:S(2)}, u32[]{:S(2)}) collective-permute-start(bf16[256,256]{1,0:T(8,128)(2,1)S(1)} %collective-permute-done.3.refs_4_), channel_id=1, source_target_pairs={{0,2},{1,3},{2,0},{3,1},{4,6},{5,7},{6,4},{7,5},{8,10},{9,11},{10,... | collective-permute-start | bytes 393224 | tf_op jit(solution)/shard_map/ppermute | solution.py:15
  15.8 0.0 collective-permute-done.refs_1_
  15.8 0.2 collective-permute-start.4
  15.9 2.0 %collective-permute-done.11.refs_12_ = bf16[256,256]{1,0:T(8,128)(2,1)S(1)} collective-permute-done((bf16[256,256]{1,0:T(8,128)(2,1)S(1)}, bf16[256,256]{1,0:T(8,128)(2,1)S(1)}, u32[]{:S(2)}, u32[]{:S(2)}) %collective-permute-start.11) | collective-permute-done | bytes 131104 | tf_op jit(solution)/shard_map/ppermute | solution.py:15
  17.9 1.6 %collective-permute-start.13 = (bf16[256,256]{1,0:T(8,128)(2,1)S(1)}, bf16[256,256]{1,0:T(8,128)(2,1)S(1)}, u32[]{:S(2)}, u32[]{:S(2)}) collective-permute-start(bf16[256,256]{1,0:T(8,128)(2,1)S(1)} %collective-permute-done.11.refs_12_), channel_id=1, source_target_pairs={{0,2},{1,3},{2,0},{3,1},{4,6},{5,7},{6,4},{7,5},{8,10},{9,11},{10,... | collective-permute-start | bytes 393224 | tf_op jit(solution)/shard_map/ppermute | solution.py:15
  19.5 0.0 collective-permute-done.9.refs_10_
  19.5 0.0 collective-permute-done.8.refs_9_
  19.5 0.5 collective-permute-start.12
  20.0 2.1 %collective-permute-done.5.refs_6_ = bf16[256,256]{1,0:T(8,128)(2,1)S(1)} collective-permute-done((bf16[256,256]{1,0:T(8,128)(2,1)S(1)}, bf16[256,256]{1,0:T(8,128)(2,1)S(1)}, u32[]{:S(2)}, u32[]{:S(2)}) %collective-permute-start.5) | collective-permute-done | bytes 131104 | tf_op jit(solution)/shard_map/ppermute | solution.py:15
  22.1 0.0 collective-permute-start.10
  22.1 0.0 collective-permute-done.4.refs_5_
  22.1 0.5 collective-permute-start.6
  22.6 1.8 %collective-permute-done.13.refs_14_ = bf16[256,256]{1,0:T(8,128)(2,1)S(1)} collective-permute-done((bf16[256,256]{1,0:T(8,128)(2,1)S(1)}, bf16[256,256]{1,0:T(8,128)(2,1)S(1)}, u32[]{:S(2)}, u32[]{:S(2)}) %collective-permute-start.13) | collective-permute-done | bytes 131104 | tf_op jit(solution)/shard_map/ppermute | solution.py:15
  24.4 0.0 collective-permute-done.10.refs_11_
  24.5 1.3 %collective-permute-done.14.refs_15_ = bf16[256,256]{1,0:T(8,128)(2,1)S(1)} collective-permute-done((bf16[256,256]{1,0:T(8,128)(2,1)S(1)}, bf16[256,256]{1,0:T(8,128)(2,1)S(1)}, u32[]{:S(2)}, u32[]{:S(2)}) %collective-permute-start.14) | collective-permute-done | bytes 131104 | tf_op jit(solution)/shard_map/ppermute | solution.py:15
  25.8 1.6 %copy-done = bf16[256,4096]{1,0:T(8,128)(2,1)S(1)} copy-done((bf16[256,4096]{1,0:T(8,128)(2,1)S(1)}, bf16[256,4096]{1,0:T(8,128)(2,1)}, u32[]{:S(2)}) %copy-start) | copy-done | bytes 2097176
  27.4 0.9 %copy-done.1 = bf16[256,256]{1,0:T(8,128)(2,1)S(1)} copy-done((bf16[256,256]{1,0:T(8,128)(2,1)S(1)}, bf16[256,256]{1,0:T(8,128)(2,1)}, u32[]{:S(2)}) %copy-start.1) | copy-done | bytes 131096
  28.3 0.7 %copy-done.3 = s32[16]{0:T(128)S(1)} copy-done((s32[16]{0:T(128)S(1)}, s32[16]{0:T(128)}, u32[]{:S(2)}) %copy-start.3) | copy-done | bytes 88
  28.9 1.6 %product.1 = (f32[256,512]{1,0:T(8,128)}, f32[128,256]{1,0:T(8,128)S(1)}, f32[128,256]{1,0:T(8,128)S(1)}) custom-call(s32[16]{0:T(128)S(1)} %copy-done.3, bf16[256,4096]{1,0:T(8,128)(2,1)S(1)} %copy-done, bf16[256,256]{1,0:T(8,128)(2,1)S(1)} %copy-done.1, bf16[256,256]{1,0:T(8,128)(2,1)S(1)} %collective-permute-done.refs_1_, ...), custom_call_target="tpu_custom_call" | custom-call | tf_op jit(solution)/shard_map/product/pallas_call | solution.py:98
  30.5 0.6 %copy-done.2 = f32[128,256]{1,0:T(8,128)} copy-done((f32[128,256]{1,0:T(8,128)}, f32[128,256]{1,0:T(8,128)S(1)}, u32[]{:S(2)}) %copy-start.2) | copy-done | bytes 131096
  31.1 1.4 %collective-permute-start.15 = (f32[128,256]{1,0:T(8,128)S(1)}, f32[128,256]{1,0:T(8,128)S(1)}, u32[]{:S(2)}, u32[]{:S(2)}) collective-permute-start(f32[128,256]{1,0:T(8,128)S(1)} %get-tuple-element.15), channel_id=1, source_target_pairs={{0,1},{1,0},{2,3},{3,2},{4,5},{5,4},{6,7},{7,6},{8,9},{9,8},{10,11... | collective-permute-start | bytes 393224 | tf_op jit(solution)/shard_map/ppermute | solution.py:15
  32.6 1.0 %collective-permute-done.15.got_ref = f32[128,256]{1,0:T(8,128)S(1)} collective-permute-done((f32[128,256]{1,0:T(8,128)S(1)}, f32[128,256]{1,0:T(8,128)S(1)}, u32[]{:S(2)}, u32[]{:S(2)}) %collective-permute-start.15) | collective-permute-done | bytes 131104 | tf_op jit(solution)/shard_map/ppermute | solution.py:15
  33.6 0.6 %copy-done.4 = f32[128,256]{1,0:T(8,128)} copy-done((f32[128,256]{1,0:T(8,128)}, f32[128,256]{1,0:T(8,128)S(1)}, u32[]{:S(2)}) %copy-start.4) | copy-done | bytes 131096
  34.2 1.7 %pieces.1 = (f32[32,256]{1,0:T(8,128)}, f32[32,256]{1,0:T(8,128)}, f32[32,256]{1,0:T(8,128)}, f32[32,256]{1,0:T(8,128)}, f32[32,256]{1,0:T(8,128)}, /*index=5*/f...) custom-call(s32[16]{0:T(128)} %coupling_ref.5, f32[128,256]{1,0:T(8,128)} %copy-done.2, f32[128,256]{1,0:T(8,128)} %copy-done.4), custom_call_target="tpu_custom_call" | custom-call | tf_op jit(solution)/shard_map/pieces/pallas_call | solution.py:113
  35.9 1.6 %collective-permute-start.16 = (f32[32,256]{1,0:T(8,128)}, f32[32,256]{1,0:T(8,128)S(1)}, u32[]{:S(2)}, u32[]{:S(2)}) collective-permute-start(f32[32,256]{1,0:T(8,128)} %get-tuple-element.17), channel_id=1, source_target_pairs={{0,2},{1,3},{2,0},{3,1},{4,6},{5,7},{6,4},{7,5},{8,10},{9,11},{10,... | collective-permute-start | bytes 98312 | tf_op jit(solution)/shard_map/ppermute | solution.py:15
  37.5 1.2 %collective-permute-start.17 = (f32[32,256]{1,0:T(8,128)}, f32[32,256]{1,0:T(8,128)S(1)}, u32[]{:S(2)}, u32[]{:S(2)}) collective-permute-start(f32[32,256]{1,0:T(8,128)} %get-tuple-element.18), channel_id=1, source_target_pairs={{0,4},{1,5},{2,6},{3,7},{4,0},{5,1},{6,2},{7,3},{8,12},{9,13},{10,... | collective-permute-start | bytes 98312 | tf_op jit(solution)/shard_map/ppermute | solution.py:15
  38.7 0.8 %collective-permute-start.18 = (f32[32,256]{1,0:T(8,128)}, f32[32,256]{1,0:T(8,128)S(1)}, u32[]{:S(2)}, u32[]{:S(2)}) collective-permute-start(f32[32,256]{1,0:T(8,128)} %get-tuple-element.19), channel_id=1, source_target_pairs={{0,6},{1,7},{2,4},{3,5},{4,2},{5,3},{6,0},{7,1},{8,14},{9,15},{10,... | collective-permute-start | bytes 98312 | tf_op jit(solution)/shard_map/ppermute | solution.py:15
  39.5 3.1 %collective-permute-start.19 = (f32[32,256]{1,0:T(8,128)}, f32[32,256]{1,0:T(8,128)S(1)}, u32[]{:S(2)}, u32[]{:S(2)}) collective-permute-start(f32[32,256]{1,0:T(8,128)} %get-tuple-element.20), channel_id=1, source_target_pairs={{0,8},{1,9},{2,10},{3,11},{4,12},{5,13},{6,14},{7,15},{8,0},{9,1},... | collective-permute-start | bytes 98312 | tf_op jit(solution)/shard_map/ppermute | solution.py:15
  42.6 1.3 %collective-permute-start.20 = (f32[32,256]{1,0:T(8,128)}, f32[32,256]{1,0:T(8,128)S(1)}, u32[]{:S(2)}, u32[]{:S(2)}) collective-permute-start(f32[32,256]{1,0:T(8,128)} %get-tuple-element.21), channel_id=1, source_target_pairs={{0,10},{1,11},{2,8},{3,9},{4,14},{5,15},{6,12},{7,13},{8,2},{9,3},... | collective-permute-start | bytes 98312 | tf_op jit(solution)/shard_map/ppermute | solution.py:15
  43.9 2.6 %collective-permute-start.21 = (f32[32,256]{1,0:T(8,128)}, f32[32,256]{1,0:T(8,128)S(1)}, u32[]{:S(2)}, u32[]{:S(2)}) collective-permute-start(f32[32,256]{1,0:T(8,128)} %get-tuple-element.22), channel_id=1, source_target_pairs={{0,12},{1,13},{2,14},{3,15},{4,8},{5,9},{6,10},{7,11},{8,4},{9,5},... | collective-permute-start | bytes 98312 | tf_op jit(solution)/shard_map/ppermute | solution.py:15
  46.5 1.2 %collective-permute-start.22 = (f32[32,256]{1,0:T(8,128)}, f32[32,256]{1,0:T(8,128)S(1)}, u32[]{:S(2)}, u32[]{:S(2)}) collective-permute-start(f32[32,256]{1,0:T(8,128)} %get-tuple-element.23), channel_id=1, source_target_pairs={{0,14},{1,15},{2,12},{3,13},{4,10},{5,11},{6,8},{7,9},{8,6},{9,7},... | collective-permute-start | bytes 98312 | tf_op jit(solution)/shard_map/ppermute | solution.py:15
  47.7 0.0 collective-permute-done.18
  47.7 0.0 collective-permute-done.19
  47.7 1.0 %collective-permute-done.20 = f32[32,256]{1,0:T(8,128)S(1)} collective-permute-done((f32[32,256]{1,0:T(8,128)}, f32[32,256]{1,0:T(8,128)S(1)}, u32[]{:S(2)}, u32[]{:S(2)}) %collective-permute-start.20) | collective-permute-done | bytes 32800 | tf_op jit(solution)/shard_map/ppermute | solution.py:15
  48.7 1.3 %collective-permute-done.21 = f32[32,256]{1,0:T(8,128)S(1)} collective-permute-done((f32[32,256]{1,0:T(8,128)}, f32[32,256]{1,0:T(8,128)S(1)}, u32[]{:S(2)}, u32[]{:S(2)}) %collective-permute-start.21) | collective-permute-done | bytes 32800 | tf_op jit(solution)/shard_map/ppermute | solution.py:15
  50.0 3.4 %collective-permute-done.22 = f32[32,256]{1,0:T(8,128)S(1)} collective-permute-done((f32[32,256]{1,0:T(8,128)}, f32[32,256]{1,0:T(8,128)S(1)}, u32[]{:S(2)}, u32[]{:S(2)}) %collective-permute-start.22) | collective-permute-done | bytes 32800 | tf_op jit(solution)/shard_map/ppermute | solution.py:15
  53.4 1.4 %add_add_fusion = f32[32,256]{1,0:T(8,128)} fusion(f32[32,256]{1,0:T(8,128)S(1)} %collective-permute-done.22, f32[32,256]{1,0:T(8,128)S(1)} %collective-permute-done.21, f32[32,256]{1,0:T(8,128)S(1)} %collective-permute-done.20, f32[32,256]{1,0:T(8,128)S(1)} %collective-permute-done.19, f32[32,256]{1,0:T(8,128)S(1)} %collective-permute-done.18, ...), kind=kLoop, calls=%fused_computation | loop fusion | flops 65536 | bytes 327680 | tf_op jit(solution)/shard_map/add | solution.py:122
  (14 shorter events, 0.0 us)
Async XLA Ops:
  0.6 52.7 %copy-start.5 = (f32[32,256]{1,0:T(8,128)S(1)}, f32[32,256]{1,0:T(8,128)}, u32[]{:S(2)}) copy-start(f32[32,256]{1,0:T(8,128)} %param.7) | copy-start | bytes 98308
  2.3 10.7 %collective-permute-start.7 = (bf16[256,256]{1,0:T(8,128)(2,1)}, bf16[256,256]{1,0:T(8,128)(2,1)S(1)}, u32[]{:S(2)}, u32[]{:S(2)}) collective-permute-start(bf16[256,256]{1,0:T(8,128)(2,1)} %compact.1.refs_0_), channel_id=1, source_target_pairs={{0,8},{1,9},{2,10},{3,11},{4,12},{5,13},{6,14},{7,15},{8,0},{9,1},... | collective-permute-start | bytes 393224 | tf_op jit(solution)/shard_map/ppermute | solution.py:15
  6.3 8.9 %collective-permute-start.3 = (bf16[256,256]{1,0:T(8,128)(2,1)}, bf16[256,256]{1,0:T(8,128)(2,1)S(1)}, u32[]{:S(2)}, u32[]{:S(2)}) collective-permute-start(bf16[256,256]{1,0:T(8,128)(2,1)} %compact.1.refs_0_), channel_id=1, source_target_pairs={{0,4},{1,5},{2,6},{3,7},{4,0},{5,1},{6,2},{7,3},{8,12},{9,13},{10,... | collective-permute-start | bytes 393224 | tf_op jit(solution)/shard_map/ppermute | solution.py:15
  7.9 7.3 %collective-permute-start.1 = (bf16[256,256]{1,0:T(8,128)(2,1)}, bf16[256,256]{1,0:T(8,128)(2,1)S(1)}, u32[]{:S(2)}, u32[]{:S(2)}) collective-permute-start(bf16[256,256]{1,0:T(8,128)(2,1)} %compact.1.refs_0_), channel_id=1, source_target_pairs={{0,2},{1,3},{2,0},{3,1},{4,6},{5,7},{6,4},{7,5},{8,10},{9,11},{10,... | collective-permute-start | bytes 393224 | tf_op jit(solution)/shard_map/ppermute | solution.py:15
  9.4 6.4 %collective-permute-start = (bf16[256,256]{1,0:T(8,128)(2,1)}, bf16[256,256]{1,0:T(8,128)(2,1)S(1)}, u32[]{:S(2)}, u32[]{:S(2)}) collective-permute-start(bf16[256,256]{1,0:T(8,128)(2,1)} %compact.1.refs_0_), channel_id=1, source_target_pairs={{0,1},{1,0},{2,3},{3,2},{4,5},{5,4},{6,7},{7,6},{8,9},{9,8},{10,11... | collective-permute-start | bytes 393224 | tf_op jit(solution)/shard_map/ppermute | solution.py:15
  12.9 5.0 %collective-permute-start.11 = (bf16[256,256]{1,0:T(8,128)(2,1)S(1)}, bf16[256,256]{1,0:T(8,128)(2,1)S(1)}, u32[]{:S(2)}, u32[]{:S(2)}) collective-permute-start(bf16[256,256]{1,0:T(8,128)(2,1)S(1)} %collective-permute-done.7.refs_8_), channel_id=1, source_target_pairs={{0,4},{1,5},{2,6},{3,7},{4,0},{5,1},{6,2},{7,3},{8,12},{9,13},{10,... | collective-permute-start | bytes 393224 | tf_op jit(solution)/shard_map/ppermute | solution.py:15
  13.7 5.8 %collective-permute-start.9 = (bf16[256,256]{1,0:T(8,128)(2,1)S(1)}, bf16[256,256]{1,0:T(8,128)(2,1)S(1)}, u32[]{:S(2)}, u32[]{:S(2)}) collective-permute-start(bf16[256,256]{1,0:T(8,128)(2,1)S(1)} %collective-permute-done.7.refs_8_), channel_id=1, source_target_pairs={{0,2},{1,3},{2,0},{3,1},{4,6},{5,7},{6,4},{7,5},{8,10},{9,11},{10,... | collective-permute-start | bytes 393224 | tf_op jit(solution)/shard_map/ppermute | solution.py:15
  15.2 4.3 %collective-permute-start.8 = (bf16[256,256]{1,0:T(8,128)(2,1)S(1)}, bf16[256,256]{1,0:T(8,128)(2,1)S(1)}, u32[]{:S(2)}, u32[]{:S(2)}) collective-permute-start(bf16[256,256]{1,0:T(8,128)(2,1)S(1)} %collective-permute-done.7.refs_8_), channel_id=1, source_target_pairs={{0,1},{1,0},{2,3},{3,2},{4,5},{5,4},{6,7},{7,6},{8,9},{9,8},{10,11... | collective-permute-start | bytes 393224 | tf_op jit(solution)/shard_map/ppermute | solution.py:15
  15.2 6.9 %collective-permute-start.5 = (bf16[256,256]{1,0:T(8,128)(2,1)S(1)}, bf16[256,256]{1,0:T(8,128)(2,1)S(1)}, u32[]{:S(2)}, u32[]{:S(2)}) collective-permute-start(bf16[256,256]{1,0:T(8,128)(2,1)S(1)} %collective-permute-done.3.refs_4_), channel_id=1, source_target_pairs={{0,2},{1,3},{2,0},{3,1},{4,6},{5,7},{6,4},{7,5},{8,10},{9,11},{10,... | collective-permute-start | bytes 393224 | tf_op jit(solution)/shard_map/ppermute | solution.py:15
  15.8 6.3 %collective-permute-start.4 = (bf16[256,256]{1,0:T(8,128)(2,1)S(1)}, bf16[256,256]{1,0:T(8,128)(2,1)S(1)}, u32[]{:S(2)}, u32[]{:S(2)}) collective-permute-start(bf16[256,256]{1,0:T(8,128)(2,1)S(1)} %collective-permute-done.3.refs_4_), channel_id=1, source_target_pairs={{0,1},{1,0},{2,3},{3,2},{4,5},{5,4},{6,7},{7,6},{8,9},{9,8},{10,11... | collective-permute-start | bytes 393224 | tf_op jit(solution)/shard_map/ppermute | solution.py:15
  17.9 6.5 %collective-permute-start.13 = (bf16[256,256]{1,0:T(8,128)(2,1)S(1)}, bf16[256,256]{1,0:T(8,128)(2,1)S(1)}, u32[]{:S(2)}, u32[]{:S(2)}) collective-permute-start(bf16[256,256]{1,0:T(8,128)(2,1)S(1)} %collective-permute-done.11.refs_12_), channel_id=1, source_target_pairs={{0,2},{1,3},{2,0},{3,1},{4,6},{5,7},{6,4},{7,5},{8,10},{9,11},{10,... | collective-permute-start | bytes 393224 | tf_op jit(solution)/shard_map/ppermute | solution.py:15
  19.5 4.9 %collective-permute-start.2 = (bf16[256,256]{1,0:T(8,128)(2,1)S(1)}, bf16[256,256]{1,0:T(8,128)(2,1)S(1)}, u32[]{:S(2)}, u32[]{:S(2)}) collective-permute-start(bf16[256,256]{1,0:T(8,128)(2,1)S(1)} %collective-permute-done.1.refs_2_), channel_id=1, source_target_pairs={{0,1},{1,0},{2,3},{3,2},{4,5},{5,4},{6,7},{7,6},{8,9},{9,8},{10,11... | collective-permute-start | bytes 393224 | tf_op jit(solution)/shard_map/ppermute | solution.py:15
  19.5 4.9 %collective-permute-start.12 = (bf16[256,256]{1,0:T(8,128)(2,1)S(1)}, bf16[256,256]{1,0:T(8,128)(2,1)S(1)}, u32[]{:S(2)}, u32[]{:S(2)}) collective-permute-start(bf16[256,256]{1,0:T(8,128)(2,1)S(1)} %collective-permute-done.11.refs_12_), channel_id=1, source_target_pairs={{0,1},{1,0},{2,3},{3,2},{4,5},{5,4},{6,7},{7,6},{8,9},{9,8},{10,11... | collective-permute-start | bytes 393224 | tf_op jit(solution)/shard_map/ppermute | solution.py:15
  22.1 2.3 %collective-permute-start.10 = (bf16[256,256]{1,0:T(8,128)(2,1)S(1)}, bf16[256,256]{1,0:T(8,128)(2,1)S(1)}, u32[]{:S(2)}, u32[]{:S(2)}) collective-permute-start(bf16[256,256]{1,0:T(8,128)(2,1)S(1)} %collective-permute-done.9.refs_10_), channel_id=1, source_target_pairs={{0,1},{1,0},{2,3},{3,2},{4,5},{5,4},{6,7},{7,6},{8,9},{9,8},{10,11... | collective-permute-start | bytes 393224 | tf_op jit(solution)/shard_map/ppermute | solution.py:15
  22.1 2.3 %collective-permute-start.6 = (bf16[256,256]{1,0:T(8,128)(2,1)S(1)}, bf16[256,256]{1,0:T(8,128)(2,1)S(1)}, u32[]{:S(2)}, u32[]{:S(2)}) collective-permute-start(bf16[256,256]{1,0:T(8,128)(2,1)S(1)} %collective-permute-done.5.refs_6_), channel_id=1, source_target_pairs={{0,1},{1,0},{2,3},{3,2},{4,5},{5,4},{6,7},{7,6},{8,9},{9,8},{10,11... | collective-permute-start | bytes 393224 | tf_op jit(solution)/shard_map/ppermute | solution.py:15
  24.4 1.3 %collective-permute-start.14 = (bf16[256,256]{1,0:T(8,128)(2,1)S(1)}, bf16[256,256]{1,0:T(8,128)(2,1)S(1)}, u32[]{:S(2)}, u32[]{:S(2)}) collective-permute-start(bf16[256,256]{1,0:T(8,128)(2,1)S(1)} %collective-permute-done.13.refs_14_), channel_id=1, source_target_pairs={{0,1},{1,0},{2,3},{3,2},{4,5},{5,4},{6,7},{7,6},{8,9},{9,8},{10,11... | collective-permute-start | bytes 393224 | tf_op jit(solution)/shard_map/ppermute | solution.py:15
  25.8 1.6 %copy-start = (bf16[256,4096]{1,0:T(8,128)(2,1)S(1)}, bf16[256,4096]{1,0:T(8,128)(2,1)}, u32[]{:S(2)}) copy-start(bf16[256,4096]{1,0:T(8,128)(2,1)} %inverse_ref.1) | copy-start | bytes 6291460
  27.4 0.9 %copy-start.1 = (bf16[256,256]{1,0:T(8,128)(2,1)S(1)}, bf16[256,256]{1,0:T(8,128)(2,1)}, u32[]{:S(2)}) copy-start(bf16[256,256]{1,0:T(8,128)(2,1)} %compact.1.refs_0_) | copy-start | bytes 393220
  28.3 0.7 %copy-start.3 = (s32[16]{0:T(128)S(1)}, s32[16]{0:T(128)}, u32[]{:S(2)}) copy-start(s32[16]{0:T(128)} %coupling_ref.5) | copy-start | bytes 196
  30.5 0.7 %copy-start.2 = (f32[128,256]{1,0:T(8,128)}, f32[128,256]{1,0:T(8,128)S(1)}, u32[]{:S(2)}) copy-start(f32[128,256]{1,0:T(8,128)S(1)} %get-tuple-element.14.keep_ref) | copy-start | bytes 393220
  31.1 2.4 %collective-permute-start.15 = (f32[128,256]{1,0:T(8,128)S(1)}, f32[128,256]{1,0:T(8,128)S(1)}, u32[]{:S(2)}, u32[]{:S(2)}) collective-permute-start(f32[128,256]{1,0:T(8,128)S(1)} %get-tuple-element.15), channel_id=1, source_target_pairs={{0,1},{1,0},{2,3},{3,2},{4,5},{5,4},{6,7},{7,6},{8,9},{9,8},{10,11... | collective-permute-start | bytes 393224 | tf_op jit(solution)/shard_map/ppermute | solution.py:15
  33.5 0.6 %copy-start.4 = (f32[128,256]{1,0:T(8,128)}, f32[128,256]{1,0:T(8,128)S(1)}, u32[]{:S(2)}) copy-start(f32[128,256]{1,0:T(8,128)S(1)} %collective-permute-done.15.got_ref) | copy-start | bytes 393220
  35.9 8.0 %collective-permute-start.16 = (f32[32,256]{1,0:T(8,128)}, f32[32,256]{1,0:T(8,128)S(1)}, u32[]{:S(2)}, u32[]{:S(2)}) collective-permute-start(f32[32,256]{1,0:T(8,128)} %get-tuple-element.17), channel_id=1, source_target_pairs={{0,2},{1,3},{2,0},{3,1},{4,6},{5,7},{6,4},{7,5},{8,10},{9,11},{10,... | collective-permute-start | bytes 98312 | tf_op jit(solution)/shard_map/ppermute | solution.py:15
  37.5 9.0 %collective-permute-start.17 = (f32[32,256]{1,0:T(8,128)}, f32[32,256]{1,0:T(8,128)S(1)}, u32[]{:S(2)}, u32[]{:S(2)}) collective-permute-start(f32[32,256]{1,0:T(8,128)} %get-tuple-element.18), channel_id=1, source_target_pairs={{0,4},{1,5},{2,6},{3,7},{4,0},{5,1},{6,2},{7,3},{8,12},{9,13},{10,... | collective-permute-start | bytes 98312 | tf_op jit(solution)/shard_map/ppermute | solution.py:15
  38.7 9.0 %collective-permute-start.18 = (f32[32,256]{1,0:T(8,128)}, f32[32,256]{1,0:T(8,128)S(1)}, u32[]{:S(2)}, u32[]{:S(2)}) collective-permute-start(f32[32,256]{1,0:T(8,128)} %get-tuple-element.19), channel_id=1, source_target_pairs={{0,6},{1,7},{2,4},{3,5},{4,2},{5,3},{6,0},{7,1},{8,14},{9,15},{10,... | collective-permute-start | bytes 98312 | tf_op jit(solution)/shard_map/ppermute | solution.py:15
  39.5 8.3 %collective-permute-start.19 = (f32[32,256]{1,0:T(8,128)}, f32[32,256]{1,0:T(8,128)S(1)}, u32[]{:S(2)}, u32[]{:S(2)}) collective-permute-start(f32[32,256]{1,0:T(8,128)} %get-tuple-element.20), channel_id=1, source_target_pairs={{0,8},{1,9},{2,10},{3,11},{4,12},{5,13},{6,14},{7,15},{8,0},{9,1},... | collective-permute-start | bytes 98312 | tf_op jit(solution)/shard_map/ppermute | solution.py:15
  42.6 6.2 %collective-permute-start.20 = (f32[32,256]{1,0:T(8,128)}, f32[32,256]{1,0:T(8,128)S(1)}, u32[]{:S(2)}, u32[]{:S(2)}) collective-permute-start(f32[32,256]{1,0:T(8,128)} %get-tuple-element.21), channel_id=1, source_target_pairs={{0,10},{1,11},{2,8},{3,9},{4,14},{5,15},{6,12},{7,13},{8,2},{9,3},... | collective-permute-start | bytes 98312 | tf_op jit(solution)/shard_map/ppermute | solution.py:15
  43.9 6.1 %collective-permute-start.21 = (f32[32,256]{1,0:T(8,128)}, f32[32,256]{1,0:T(8,128)S(1)}, u32[]{:S(2)}, u32[]{:S(2)}) collective-permute-start(f32[32,256]{1,0:T(8,128)} %get-tuple-element.22), channel_id=1, source_target_pairs={{0,12},{1,13},{2,14},{3,15},{4,8},{5,9},{6,10},{7,11},{8,4},{9,5},... | collective-permute-start | bytes 98312 | tf_op jit(solution)/shard_map/ppermute | solution.py:15
  46.5 6.8 %collective-permute-start.22 = (f32[32,256]{1,0:T(8,128)}, f32[32,256]{1,0:T(8,128)S(1)}, u32[]{:S(2)}, u32[]{:S(2)}) collective-permute-start(f32[32,256]{1,0:T(8,128)} %get-tuple-element.23), channel_id=1, source_target_pairs={{0,14},{1,15},{2,12},{3,13},{4,10},{5,11},{6,8},{7,9},{8,6},{9,7},... | collective-permute-start | bytes 98312 | tf_op jit(solution)/shard_map/ppermute | solution.py:15

commit v2 on v1

v2 whole, which is shorter than its diff:
```python
import functools

import jax
import jax.numpy as jnp
from jax import lax
from jax.experimental import pallas as pl
from jax.experimental.pallas import tpu as pltpu
from jax.sharding import PartitionSpec as P

NCH = 2
CW = 256
MIB = 2**20
QUAD = ((0, 0), (1, 2), (2, 1), (3, 3))
SMEM = pl.BlockSpec(memory_space=pltpu.SMEM)
VMEM = pl.BlockSpec(memory_space=pltpu.VMEM)
ANY = pl.BlockSpec(memory_space=pl.ANY)


def params(mib):
    return pltpu.CompilerParams(vmem_limit_bytes=mib * MIB)


def exchange(block, n, masks):
    return lax.ppermute(block, "row", [(i, i ^ masks[i % 2]) for i in range(n)])


def compact_kernel(coupling_ref, panel_ref, block_ref):
    child = coupling_ref[lax.axis_index("row")]
    start = pl.multiple_of(jnp.minimum(child, NCH - 1) * CW, CW)
    block_ref[...] = panel_ref[:, pl.ds(start, CW)]


def load_kernel(inverse_hbm, after_ref, inverse_ref, sem):
    copy = pltpu.make_async_copy(inverse_hbm, inverse_ref, sem)
    copy.start()
    copy.wait()


def after_kernel(block_ref, after_ref, out_ref):
    out_ref[...] = block_ref[...]


def join_kernel(low_ref, high_ref, after_ref, out_ref):
    rows = low_ref.shape[0]
    out_ref[:rows] = low_ref[...]
    out_ref[rows:] = high_ref[...]


def late_kernel(n, places, coupling_ref, inverse_ref, *refs):
    rows = inverse_ref.shape[0]
    block_refs = refs[:-4]
    product_ref, send_ref, keep_ref, flag_ref = refs[-4:]
    me = lax.axis_index("row")
    core = lax.rem(me, 2)
    child = coupling_ref[me]
    other = coupling_ref[me ^ 1]
    product_ref[...] = jnp.zeros_like(product_ref)
    for held, block_ref in zip(places, block_refs):
        for number, (even, odd) in enumerate(held):
            tile = me ^ jnp.where(core == 0, even, odd)

            @pl.when((coupling_ref[tile] == child) & (child < NCH))
            def _():
                start = pl.multiple_of(tile * rows, rows)
                product_ref[...] += jnp.dot(
                    inverse_ref[:, pl.ds(start, rows)],
                    block_ref[number * rows:(number + 1) * rows],
                    preferred_element_type=jnp.float32,
                )

    left = block_refs[0][...]
    rest = product_ref[...]
    term = jnp.zeros_like(rest)
    for _ in range(3):
        part = rest.astype(jnp.bfloat16)
        rest = rest - part.astype(jnp.float32)
        term += lax.dot_general(
            left, part, (((0,), (0,)), ((), ())), preferred_element_type=jnp.float32
        )
    piece = NCH * CW // n
    for q in range(CW // piece // 2):
        low = term[2 * q * piece:(2 * q + 1) * piece]
        high = term[(2 * q + 1) * piece:(2 * q + 2) * piece]
        keep_ref[q * piece:(q + 1) * piece] = jnp.where(core == 0, low, high)
        send_ref[q * piece:(q + 1) * piece] = jnp.where(core == 0, high, low)
    for k in range(NCH):
        flag_ref[2 * k:2 * k + 1] = jnp.full((1, CW), jnp.where(child == k, 1.0, 0.0))
        flag_ref[2 * k + 1:2 * k + 2] = jnp.full(
            (1, CW), jnp.where(other == k, 1.0, 0.0)
        )


def offdiag_kernel(coupling_ref, product_ref, offdiag_ref):
    child = coupling_ref[lax.axis_index("row")]
    product = product_ref[...]
    for k in range(NCH):
        offdiag_ref[:, k * CW:(k + 1) * CW] = jnp.where(
            child == k, -product, jnp.zeros_like(product)
        )


def quad_kernel(piece, kept_ref, got_ref, flag_ref, *out_refs):
    me = lax.axis_index("row")
    core = lax.rem(me, 2)
    low = lax.rem(lax.div(me, 2), 4)
    groups = kept_ref.shape[0] // piece // 4
    for (even, odd), out_ref in zip(QUAD, out_refs):
        want = low ^ jnp.where(core == 0, even, odd)
        for child in range(NCH):
            for group in range(groups):
                start = pl.multiple_of((group * 4 + want) * piece, piece)
                kept = kept_ref[pl.ds(start, piece)]
                got = got_ref[pl.ds(start, piece)]
                zero = jnp.zeros_like(kept)
                at = (child * groups + group) * piece
                out_ref[at:at + piece] = jnp.where(
                    flag_ref[2 * child:2 * child + 1] > 0.5, kept, zero
                ) + jnp.where(flag_ref[2 * child + 1:2 * child + 2] > 0.5, got, zero)


def halve_kernel(piece, bit, *refs):
    part_refs, send_ref, keep_ref = refs[:-2], refs[-2], refs[-1]
    mine = lax.rem(lax.div(lax.axis_index("row"), 2 << bit), 2)
    for out_ref, side in ((keep_ref, mine), (send_ref, 1 - mine)):
        for index in range(out_ref.shape[0] // piece):
            rows = pl.ds(pl.multiple_of((2 * index + side) * piece, piece), piece)
            total = part_refs[0][rows]
            for part_ref in part_refs[1:]:
                total = total + part_ref[rows]
            out_ref[index * piece:(index + 1) * piece] = total


def last_kernel(inverse_ref, kept_ref, got_ref, diag_ref):
    diag_ref[...] = inverse_ref[...] + (kept_ref[...] + got_ref[...])


def gather(block, inverse_root, n):
    held = {"own": block}
    places = {"own": [(0, 0)]}

    def fetch(name, source, masks, block=None):
        held[name] = exchange(held[source] if block is None else block, n, masks)
        places[name] = [
            tuple(masks[c] ^ pair[c ^ (masks[0] & 1)] for c in range(2))
            for pair in places[source]
        ]

    def after(name, block):
        return pl.pallas_call(
            after_kernel,
            out_shape=pltpu.VMEM(block.shape, block.dtype),
            in_specs=[VMEM, ANY],
            out_specs=VMEM,
            compiler_params=params(2),
            name="after",
        )(block, held[name])

    fetch("d", "own", (8, 8))
    fetch("own1", "own", (1, 1))
    fetch("a", "own", (2, 4))
    inverse = pl.pallas_call(
        load_kernel,
        out_shape=pltpu.VMEM(inverse_root.shape, inverse_root.dtype),
        in_specs=[ANY, ANY],
        out_specs=VMEM,
        scratch_shapes=[pltpu.SemaphoreType.DMA],
        compiler_params=params(62 - inverse_root.size * 2 // MIB),
        name="load",
    )(inverse_root, held["own1"])
    pair = pl.pallas_call(
        join_kernel,
        out_shape=pltpu.VMEM((2 * block.shape[0], CW), block.dtype),
        in_specs=[VMEM, VMEM, ANY],
        out_specs=VMEM,
        compiler_params=params(2),
        name="join",
    )(block, held["a"], inverse)
    places["pair"] = places["own"] + places["a"]
    fetch("bc", "pair", (4, 2), pair)
    del places["pair"]
    fetch("a1", "a", (1, 1))
    fetch("d1", "d", (1, 1))
    fetch("f", "d", (2, 4))
    fetch("e", "d", (4, 2))
    fetch("g", "d", (6, 6), after("d1", held["d"]))
    for name in ("bc", "f", "e", "g"):
        fetch(name + "1", name, (1, 1))
    for bit in range(4, n.bit_length() - 1):
        for name in list(held):
            fetch(f"{name}_{bit}", name, (1 << bit, 1 << bit))
    held["inverse"] = inverse
    return held, places


def per_device(n, inverse_root, lower_panel, coupling, child_inverse):
    rows = inverse_root.shape[0]
    block = pl.pallas_call(
        compact_kernel,
        out_shape=pltpu.VMEM((rows, CW), lower_panel.dtype),
        in_specs=[SMEM, VMEM],
        out_specs=VMEM,
        compiler_params=params(60),
        name="compact",
    )(coupling, lower_panel)
    held, places = gather(block, inverse_root, n)
    inverse = held.pop("inverse")
    product, send, keep, flags = pl.pallas_call(
        functools.partial(late_kernel, n, list(places.values())),
        out_shape=[
            jax.ShapeDtypeStruct((rows, CW), jnp.float32),
            jax.ShapeDtypeStruct((CW // 2, CW), jnp.float32),
            jax.ShapeDtypeStruct((CW // 2, CW), jnp.float32),
            jax.ShapeDtypeStruct((8, CW), jnp.float32),
        ],
        in_specs=[SMEM] + [VMEM] * (len(held) + 1),
        out_specs=[VMEM] * 4,
        compiler_params=params(24 if n > 16 else 8),
        name="late",
    )(coupling, inverse, *held.values())
    got = exchange(send, n, (1, 1))
    offdiag = pl.pallas_call(
        offdiag_kernel,
        out_shape=jax.ShapeDtypeStruct((rows, NCH * CW), jnp.float32),
        in_specs=[SMEM, VMEM],
        out_specs=VMEM,
        compiler_params=params(2),
        name="offdiag",
    )(coupling, product)
    piece = NCH * CW // n
    width = NCH * CW // 2 // len(QUAD)
    parts = list(pl.pallas_call(
        functools.partial(quad_kernel, piece),
        out_shape=[jax.ShapeDtypeStruct((width, CW), jnp.float32)] * len(QUAD),
        in_specs=[VMEM] * 3,
        out_specs=[VMEM] * len(QUAD),
        compiler_params=params(2),
        name="quad",
    )(keep, got, flags))
    for number in range(1, len(QUAD)):
        parts[number] = exchange(parts[number], n, tuple(2 * m for m in QUAD[number]))
    for bit in range(2, (n // 2).bit_length() - 1):
        width //= 2
        send, keep = pl.pallas_call(
            functools.partial(halve_kernel, piece, bit),
            out_shape=[jax.ShapeDtypeStruct((width, CW), jnp.float32)] * 2,
            in_specs=[VMEM] * len(parts),
            out_specs=[VMEM] * 2,
            compiler_params=params(2),
            name=f"halve{bit}",
        )(*parts)
        got = exchange(send, n, (2 << bit, 2 << bit))
        parts = [keep, got]
    child_diag = pl.pallas_call(
        last_kernel,
        out_shape=jax.ShapeDtypeStruct((piece, CW), jnp.float32),
        in_specs=[VMEM] * 3,
        out_specs=VMEM,
        compiler_params=params(2),
        name="last",
    )(child_inverse, keep, got)
    return offdiag, child_diag


def solution(mesh):
    split = P(("pole", "row"), None)
    return jax.shard_map(
        functools.partial(per_device, mesh.shape["row"]),
        mesh=mesh,
        in_specs=(split, split, P(), split),
        out_specs=(split, split),
        check_vma=False,
    )
```

time: 54.9 us -> 40.4 us (0.74)
  starting transfers between devices: 25.9 us -> 19 us
  local copies, waits for them, and re-layouts: 4.45 us -> 0.67 us
  waiting for transfers between devices: 17.4 us -> 14 us
  other arithmetic: 1.39 us -> 0 us
  Pallas kernels: 4.93 us -> 5.67 us
    ppermute x23 -> x18, starting transfers between devices: 25.9 us -> 19 us  [exchange(): return lax.ppermute(block, 'row', [(i, i ^ masks[i % 2]) for i in range(n)])]
    unnamed x12 -> x8, local copies, waits for them, and re-layouts: 4.45 us -> 0.67 us
    ppermute x23 -> x18, waiting for transfers between devices: 17.4 us -> 14 us  [exchange(): return lax.ppermute(block, 'row', [(i, i ^ masks[i % 2]) for i in range(n)])]
    add x1 -> x0, other arithmetic: 1.39 us -> none  [per_device(): child_diag = child_diag + exchange(parts[offset], n, 2 * offset)]
    pallas_call x3 -> x9, Pallas kernels: 4.93 us -> 5.67 us  [the longest x1 1.6 us: gather(): pl.pallas_call(load_kernel, out_shape=pltpu.VMEM(inverse_root.shape, inve...]
  transfers between devices with their start and end apart: 23 -> 18, of which waited for: 9 -> 10; matrix products, arithmetic and copies ran while one was open for 0% -> 0% of each run, Pallas kernels for 0% -> 8%
where the time goes in v2:
time: 40.4 us; the launch traced here: 40.1 us
  starting transfers between devices  19 us (47%)
  waiting for transfers between devices  14 us (35%)
  Pallas kernels  5.67 us (14%)
  between operations  0.73 us (2%)
  local copies, waits for them, and re-layouts  0.67 us (2%)
    ppermute x18, starting transfers between devices, exchange(): return lax.ppermute(block, 'row', [(i, i ^ masks[i % 2]) for i in range(n)])  19 us
    ppermute x18, waiting for transfers between devices, exchange(): return lax.ppermute(block, 'row', [(i, i ^ masks[i % 2]) for i in range(n)])  14 us
    pallas_call x1, Pallas kernels, gather(): pl.pallas_call(load_kernel, out_shape=pltpu.VMEM(inverse_root.shape, inve...  1.6 us
    pallas_call x1, Pallas kernels, per_device(): pl.pallas_call(offdiag_kernel, out_shape=jax.ShapeDtypeStruct((rows, NCH...  1.38 us
    pallas_call x1, Pallas kernels, per_device(): pl.pallas_call(functools.partial(late_kernel, n, list(places.values())),...  1 us
    pallas_call x1, Pallas kernels, per_device(): pl.pallas_call(compact_kernel, out_shape=pltpu.VMEM((rows, CW), lower_pan...  0.98 us
  transfers between devices with their start and end apart: 18, of which 10 were waited for; matrix products, arithmetic and copies ran while one was open for 0% of the time, Pallas kernels for 8%

profile of v2, /device:TPU:0, one launch (start us, length us, event | category | flops | bytes accessed | tf_op | source)
XLA Modules:
  0.0 40.1 jit_solution(6575115522642160748)
XLA Ops:
  0.6 1.0 %compact.1.low_ref.refs_0_ = bf16[256,256]{1,0:T(8,128)(2,1)S(1)} custom-call(s32[16]{0:T(128)} %coupling_ref.5, bf16[256,512]{1,0:T(8,128)(2,1)} %panel_ref.1), custom_call_target="tpu_custom_call" | custom-call | tf_op jit(solution)/shard_map/compact/pallas_call | solution.py:197
  1.6 0.5 %collective-permute-start = (bf16[256,256]{1,0:T(8,128)(2,1)S(1)}, bf16[256,256]{1,0:T(8,128)(2,1)S(1)}, u32[]{:S(2)}, u32[]{:S(2)}) collective-permute-start(bf16[256,256]{1,0:T(8,128)(2,1)S(1)} %compact.1.low_ref.refs_0_), channel_id=1, source_target_pairs={{0,1},{1,0},{2,3},{3,2},{4,5},{5,4},{6,7},{7,6},{8,9},{9,8},{10,11... | collective-permute-start | bytes 393224 | tf_op jit(solution)/shard_map/ppermute | solution.py:24
  2.1 2.6 %collective-permute-start.2 = (bf16[256,256]{1,0:T(8,128)(2,1)S(1)}, bf16[256,256]{1,0:T(8,128)(2,1)S(1)}, u32[]{:S(2)}, u32[]{:S(2)}) collective-permute-start(bf16[256,256]{1,0:T(8,128)(2,1)S(1)} %compact.1.low_ref.refs_0_), channel_id=1, source_target_pairs={{0,2},{1,5},{2,0},{3,7},{4,6},{5,1},{6,4},{7,3},{8,10},{9,13},{10,... | collective-permute-start | bytes 393224 | tf_op jit(solution)/shard_map/ppermute | solution.py:24
  4.7 2.6 %collective-permute-start.1 = (bf16[256,256]{1,0:T(8,128)(2,1)S(1)}, bf16[256,256]{1,0:T(8,128)(2,1)S(1)}, u32[]{:S(2)}, u32[]{:S(2)}) collective-permute-start(bf16[256,256]{1,0:T(8,128)(2,1)S(1)} %compact.1.low_ref.refs_0_), channel_id=1, source_target_pairs={{0,8},{1,9},{2,10},{3,11},{4,12},{5,13},{6,14},{7,15},{8,0},{9,1},... | collective-permute-start | bytes 393224 | tf_op jit(solution)/shard_map/ppermute | solution.py:24
  7.3 0.0 collective-permute-done.after_ref.refs_2_
  7.3 0.7 %copy-done = bf16[256,256]{1,0:T(8,128)(2,1)} copy-done((bf16[256,256]{1,0:T(8,128)(2,1)}, bf16[256,256]{1,0:T(8,128)(2,1)S(1)}, u32[]{:S(2)}) %copy-start) | copy-done | bytes 131096
  8.0 1.6 %load.1.after_ref.inverse_ref = bf16[256,4096]{1,0:T(8,128)(2,1)S(1)} custom-call(bf16[256,4096]{1,0:T(8,128)(2,1)} %inverse_hbm.1, bf16[256,256]{1,0:T(8,128)(2,1)} %copy-done), custom_call_target="tpu_custom_call" | custom-call | tf_op jit(solution)/shard_map/load/pallas_call | solution.py:161
  9.6 0.0 copy-start.1
  9.6 0.0 copy-start.3
  9.6 0.0 collective-permute-done.2.high_ref.refs_3_
  9.7 1.6 %collective-permute-start.3 = (bf16[512,256]{1,0:T(8,128)(2,1)S(1)}, bf16[512,256]{1,0:T(8,128)(2,1)S(1)}, u32[]{:S(2)}, u32[]{:S(2)}) collective-permute-start(bf16[512,256]{1,0:T(8,128)(2,1)S(1)} %join.1), channel_id=1, source_target_pairs={{0,4},{1,3},{2,6},{3,1},{4,0},{5,7},{6,2},{7,5},{8,12},{9,11},{10,... | collective-permute-start | bytes 786440 | tf_op jit(solution)/shard_map/ppermute | solution.py:24
  11.3 2.8 %collective-permute-done.1.block_ref.refs_1_ = bf16[256,256]{1,0:T(8,128)(2,1)S(1)} collective-permute-done((bf16[256,256]{1,0:T(8,128)(2,1)S(1)}, bf16[256,256]{1,0:T(8,128)(2,1)S(1)}, u32[]{:S(2)}, u32[]{:S(2)}) %collective-permute-start.1) | collective-permute-done | bytes 131104 | tf_op jit(solution)/shard_map/ppermute | solution.py:24
  14.1 0.0 collective-permute-start.5
  14.1 0.0 collective-permute-start.7
  14.1 1.1 %collective-permute-start.6 = (bf16[256,256]{1,0:T(8,128)(2,1)S(1)}, bf16[256,256]{1,0:T(8,128)(2,1)S(1)}, u32[]{:S(2)}, u32[]{:S(2)}) collective-permute-start(bf16[256,256]{1,0:T(8,128)(2,1)S(1)} %collective-permute-done.1.block_ref.refs_1_), channel_id=1, source_target_pairs={{0,2},{1,5},{2,0},{3,7},{4,6},{5,1},{6,4},{7,3},{8,10},{9,13},{10,... | collective-permute-start | bytes 393224 | tf_op jit(solution)/shard_map/ppermute | solution.py:24
  15.2 0.2 collective-permute-done.5.after_ref.refs_6_
  15.5 0.0 copy-start.2
  15.5 2.2 %collective-permute-start.8 = (bf16[256,256]{1,0:T(8,128)(2,1)S(1)}, bf16[256,256]{1,0:T(8,128)(2,1)S(1)}, u32[]{:S(2)}, u32[]{:S(2)}) collective-permute-start(bf16[256,256]{1,0:T(8,128)(2,1)S(1)} %after.1), channel_id=1, source_target_pairs={{0,6},{1,7},{2,4},{3,5},{4,2},{5,3},{6,0},{7,1},{8,14},{9,15},{10,... | collective-permute-start | bytes 393224 | tf_op jit(solution)/shard_map/ppermute | solution.py:24
  17.7 0.0 collective-permute-done.3.refs_4_
  17.7 0.0 collective-permute-start.9
  17.7 0.5 %collective-permute-start.4 = (bf16[256,256]{1,0:T(8,128)(2,1)S(1)}, bf16[256,256]{1,0:T(8,128)(2,1)S(1)}, u32[]{:S(2)}, u32[]{:S(2)}) collective-permute-start(bf16[256,256]{1,0:T(8,128)(2,1)S(1)} %collective-permute-done.2.high_ref.refs_3_), channel_id=1, source_target_pairs={{0,1},{1,0},{2,3},{3,2},{4,5},{5,4},{6,7},{7,6},{8,9},{9,8},{10,11... | collective-permute-start | bytes 393224 | tf_op jit(solution)/shard_map/ppermute | solution.py:24
  18.2 2.3 %collective-permute-done.7.refs_8_ = bf16[256,256]{1,0:T(8,128)(2,1)S(1)} collective-permute-done((bf16[256,256]{1,0:T(8,128)(2,1)S(1)}, bf16[256,256]{1,0:T(8,128)(2,1)S(1)}, u32[]{:S(2)}, u32[]{:S(2)}) %collective-permute-start.7) | collective-permute-done | bytes 131104 | tf_op jit(solution)/shard_map/ppermute | solution.py:24
  20.5 0.0 collective-permute-start.11
  20.5 0.0 collective-permute-done.6.refs_7_
  20.5 0.5 %collective-permute-start.10 = (bf16[256,256]{1,0:T(8,128)(2,1)S(1)}, bf16[256,256]{1,0:T(8,128)(2,1)S(1)}, u32[]{:S(2)}, u32[]{:S(2)}) collective-permute-start(bf16[256,256]{1,0:T(8,128)(2,1)S(1)} %collective-permute-done.6.refs_7_), channel_id=1, source_target_pairs={{0,1},{1,0},{2,3},{3,2},{4,5},{5,4},{6,7},{7,6},{8,9},{9,8},{10,11... | collective-permute-start | bytes 393224 | tf_op jit(solution)/shard_map/ppermute | solution.py:24
  21.0 2.1 %collective-permute-done.8.refs_9_ = bf16[256,256]{1,0:T(8,128)(2,1)S(1)} collective-permute-done((bf16[256,256]{1,0:T(8,128)(2,1)S(1)}, bf16[256,256]{1,0:T(8,128)(2,1)S(1)}, u32[]{:S(2)}, u32[]{:S(2)}) %collective-permute-start.8) | collective-permute-done | bytes 131104 | tf_op jit(solution)/shard_map/ppermute | solution.py:24
  23.1 0.3 collective-permute-start.12
  23.4 0.0 collective-permute-done.4.refs_5_
  23.4 0.0 collective-permute-done.11.refs_12_
  23.4 0.0 collective-permute-done.10.refs_11_
  23.4 1.1 %collective-permute-done.12.refs_13_ = bf16[256,256]{1,0:T(8,128)(2,1)S(1)} collective-permute-done((bf16[256,256]{1,0:T(8,128)(2,1)S(1)}, bf16[256,256]{1,0:T(8,128)(2,1)S(1)}, u32[]{:S(2)}, u32[]{:S(2)}) %collective-permute-start.12) | collective-permute-done | bytes 131104 | tf_op jit(solution)/shard_map/ppermute | solution.py:24
  24.4 0.0 collective-permute-done.9.refs_10_
  24.4 0.0 copy-done.1
  24.4 0.0 copy-done.3
  24.5 1.0 %late.1 = (f32[256,256]{1,0:T(8,128)S(1)}, f32[128,256]{1,0:T(8,128)S(1)}, f32[128,256]{1,0:T(8,128)S(1)}, f32[8,256]{1,0:T(8,128)S(1)}) custom-call(s32[16]{0:T(128)S(1)} %copy-done.3, bf16[256,4096]{1,0:T(8,128)(2,1)S(1)} %load.1.after_ref.inverse_ref, bf16[256,256]{1,0:T(8,128)(2,1)S(1)} %compact.1.low_ref.refs_0_, ...), custom_call_target="tpu_custom_call" | custom-call | tf_op jit(solution)/shard_map/late/pallas_call | solution.py:207
  25.5 0.3 collective-permute-start.13
  25.8 1.1 %collective-permute-done.13.got_ref = f32[128,256]{1,0:T(8,128)S(1)} collective-permute-done((f32[128,256]{1,0:T(8,128)S(1)}, f32[128,256]{1,0:T(8,128)S(1)}, u32[]{:S(2)}, u32[]{:S(2)}) %collective-permute-start.13) | collective-permute-done | bytes 131104 | tf_op jit(solution)/shard_map/ppermute | solution.py:24
  26.9 2.4 %collective-permute-start.14 = (f32[64,256]{1,0:T(8,128)S(1)}, f32[64,256]{1,0:T(8,128)S(1)}, u32[]{:S(2)}, u32[]{:S(2)}) collective-permute-start(f32[64,256]{1,0:T(8,128)S(1)} %get-tuple-element.17), channel_id=1, source_target_pairs={{0,2},{1,5},{2,0},{3,7},{4,6},{5,1},{6,4},{7,3},{8,10},{9,13},{10,... | collective-permute-start | bytes 196616 | tf_op jit(solution)/shard_map/ppermute | solution.py:24
  29.3 0.1 collective-permute-start.15
  29.4 1.4 %collective-permute-start.16 = (f32[64,256]{1,0:T(8,128)S(1)}, f32[64,256]{1,0:T(8,128)S(1)}, u32[]{:S(2)}, u32[]{:S(2)}) collective-permute-start(f32[64,256]{1,0:T(8,128)S(1)} %get-tuple-element.19), channel_id=1, source_target_pairs={{0,6},{1,7},{2,4},{3,5},{4,2},{5,3},{6,0},{7,1},{8,14},{9,15},{10,... | collective-permute-start | bytes 196616 | tf_op jit(solution)/shard_map/ppermute | solution.py:24
  30.8 1.1 %collective-permute-done.14.refs_1_ = f32[64,256]{1,0:T(8,128)S(1)} collective-permute-done((f32[64,256]{1,0:T(8,128)S(1)}, f32[64,256]{1,0:T(8,128)S(1)}, u32[]{:S(2)}, u32[]{:S(2)}) %collective-permute-start.14) | collective-permute-done | bytes 65568 | tf_op jit(solution)/shard_map/ppermute | solution.py:24
  31.9 1.9 %collective-permute-done.15.refs_2_ = f32[64,256]{1,0:T(8,128)S(1)} collective-permute-done((f32[64,256]{1,0:T(8,128)S(1)}, f32[64,256]{1,0:T(8,128)S(1)}, u32[]{:S(2)}, u32[]{:S(2)}) %collective-permute-start.15) | collective-permute-done | bytes 65568 | tf_op jit(solution)/shard_map/ppermute | solution.py:24
  33.8 0.8 %collective-permute-done.16.refs_3_ = f32[64,256]{1,0:T(8,128)S(1)} collective-permute-done((f32[64,256]{1,0:T(8,128)S(1)}, f32[64,256]{1,0:T(8,128)S(1)}, u32[]{:S(2)}, u32[]{:S(2)}) %collective-permute-start.16) | collective-permute-done | bytes 65568 | tf_op jit(solution)/shard_map/ppermute | solution.py:24
  34.6 2.8 %collective-permute-start.17 = (f32[32,256]{1,0:T(8,128)S(1)}, f32[32,256]{1,0:T(8,128)S(1)}, u32[]{:S(2)}, u32[]{:S(2)}) collective-permute-start(f32[32,256]{1,0:T(8,128)S(1)} %get-tuple-element.21), channel_id=1, source_target_pairs={{0,8},{1,9},{2,10},{3,11},{4,12},{5,13},{6,14},{7,15},{8,0},{9,1},... | collective-permute-start | bytes 98312 | tf_op jit(solution)/shard_map/ppermute | solution.py:24
  37.4 1.4 %offdiag.1 = f32[256,512]{1,0:T(8,128)} custom-call(s32[16]{0:T(128)S(1)} %copy-done.3, f32[256,256]{1,0:T(8,128)S(1)} %get-tuple-element.12.product_ref), custom_call_target="tpu_custom_call" | custom-call | tf_op jit(solution)/shard_map/offdiag/pallas_call | solution.py:221
  38.8 0.7 %collective-permute-done.17.got_ref = f32[32,256]{1,0:T(8,128)S(1)} collective-permute-done((f32[32,256]{1,0:T(8,128)S(1)}, f32[32,256]{1,0:T(8,128)S(1)}, u32[]{:S(2)}, u32[]{:S(2)}) %collective-permute-start.17) | collective-permute-done | bytes 32800 | tf_op jit(solution)/shard_map/ppermute | solution.py:24
  39.4 0.0 copy-done.2
  39.4 0.6 %last.1 = f32[32,256]{1,0:T(8,128)} custom-call(f32[32,256]{1,0:T(8,128)S(1)} %copy-done.2, f32[32,256]{1,0:T(8,128)S(1)} %get-tuple-element.20.kept_ref, f32[32,256]{1,0:T(8,128)S(1)} %collective-permute-done.17.got_ref), custom_call_target="tpu_custom_call" | custom-call | tf_op jit(solution)/shard_map/last/pallas_call | solution.py:253
  (5 shorter events, 0.1 us)
Async XLA Ops:
  1.6 5.7 %collective-permute-start = (bf16[256,256]{1,0:T(8,128)(2,1)S(1)}, bf16[256,256]{1,0:T(8,128)(2,1)S(1)}, u32[]{:S(2)}, u32[]{:S(2)}) collective-permute-start(bf16[256,256]{1,0:T(8,128)(2,1)S(1)} %compact.1.low_ref.refs_0_), channel_id=1, source_target_pairs={{0,1},{1,0},{2,3},{3,2},{4,5},{5,4},{6,7},{7,6},{8,9},{9,8},{10,11... | collective-permute-start | bytes 393224 | tf_op jit(solution)/shard_map/ppermute | solution.py:24
  2.1 7.5 %collective-permute-start.2 = (bf16[256,256]{1,0:T(8,128)(2,1)S(1)}, bf16[256,256]{1,0:T(8,128)(2,1)S(1)}, u32[]{:S(2)}, u32[]{:S(2)}) collective-permute-start(bf16[256,256]{1,0:T(8,128)(2,1)S(1)} %compact.1.low_ref.refs_0_), channel_id=1, source_target_pairs={{0,2},{1,5},{2,0},{3,7},{4,6},{5,1},{6,4},{7,3},{8,10},{9,13},{10,... | collective-permute-start | bytes 393224 | tf_op jit(solution)/shard_map/ppermute | solution.py:24
  4.7 9.4 %collective-permute-start.1 = (bf16[256,256]{1,0:T(8,128)(2,1)S(1)}, bf16[256,256]{1,0:T(8,128)(2,1)S(1)}, u32[]{:S(2)}, u32[]{:S(2)}) collective-permute-start(bf16[256,256]{1,0:T(8,128)(2,1)S(1)} %compact.1.low_ref.refs_0_), channel_id=1, source_target_pairs={{0,8},{1,9},{2,10},{3,11},{4,12},{5,13},{6,14},{7,15},{8,0},{9,1},... | collective-permute-start | bytes 393224 | tf_op jit(solution)/shard_map/ppermute | solution.py:24
  7.3 0.7 %copy-start = (bf16[256,256]{1,0:T(8,128)(2,1)}, bf16[256,256]{1,0:T(8,128)(2,1)S(1)}, u32[]{:S(2)}) copy-start(bf16[256,256]{1,0:T(8,128)(2,1)S(1)} %collective-permute-done.after_ref.refs_2_) | copy-start | bytes 393220
  9.6 14.9 %copy-start.1 = (bf16[256,256]{1,0:T(8,128)(2,1)S(1)}, bf16[256,256]{1,0:T(8,128)(2,1)}, u32[]{:S(2)}) copy-start(bf16[256,256]{1,0:T(8,128)(2,1)} %copy-done) | copy-start | bytes 393220
  9.6 14.8 %copy-start.3 = (s32[16]{0:T(128)S(1)}, s32[16]{0:T(128)}, u32[]{:S(2)}) copy-start(s32[16]{0:T(128)} %coupling_ref.5) | copy-start | bytes 196
  9.7 8.1 %collective-permute-start.3 = (bf16[512,256]{1,0:T(8,128)(2,1)S(1)}, bf16[512,256]{1,0:T(8,128)(2,1)S(1)}, u32[]{:S(2)}, u32[]{:S(2)}) collective-permute-start(bf16[512,256]{1,0:T(8,128)(2,1)S(1)} %join.1), channel_id=1, source_target_pairs={{0,4},{1,3},{2,6},{3,1},{4,0},{5,7},{6,2},{7,5},{8,12},{9,11},{10,... | collective-permute-start | bytes 786440 | tf_op jit(solution)/shard_map/ppermute | solution.py:24
  14.1 1.3 %collective-permute-start.5 = (bf16[256,256]{1,0:T(8,128)(2,1)S(1)}, bf16[256,256]{1,0:T(8,128)(2,1)S(1)}, u32[]{:S(2)}, u32[]{:S(2)}) collective-permute-start(bf16[256,256]{1,0:T(8,128)(2,1)S(1)} %collective-permute-done.1.block_ref.refs_1_), channel_id=1, source_target_pairs={{0,1},{1,0},{2,3},{3,2},{4,5},{5,4},{6,7},{7,6},{8,9},{9,8},{10,11... | collective-permute-start | bytes 393224 | tf_op jit(solution)/shard_map/ppermute | solution.py:24
  14.1 6.4 %collective-permute-start.7 = (bf16[256,256]{1,0:T(8,128)(2,1)S(1)}, bf16[256,256]{1,0:T(8,128)(2,1)S(1)}, u32[]{:S(2)}, u32[]{:S(2)}) collective-permute-start(bf16[256,256]{1,0:T(8,128)(2,1)S(1)} %collective-permute-done.1.block_ref.refs_1_), channel_id=1, source_target_pairs={{0,4},{1,3},{2,6},{3,1},{4,0},{5,7},{6,2},{7,5},{8,12},{9,11},{10,... | collective-permute-start | bytes 393224 | tf_op jit(solution)/shard_map/ppermute | solution.py:24
  14.1 6.4 %collective-permute-start.6 = (bf16[256,256]{1,0:T(8,128)(2,1)S(1)}, bf16[256,256]{1,0:T(8,128)(2,1)S(1)}, u32[]{:S(2)}, u32[]{:S(2)}) collective-permute-start(bf16[256,256]{1,0:T(8,128)(2,1)S(1)} %collective-permute-done.1.block_ref.refs_1_), channel_id=1, source_target_pairs={{0,2},{1,5},{2,0},{3,7},{4,6},{5,1},{6,4},{7,3},{8,10},{9,13},{10,... | collective-permute-start | bytes 393224 | tf_op jit(solution)/shard_map/ppermute | solution.py:24
  15.5 23.9 %copy-start.2 = (f32[32,256]{1,0:T(8,128)S(1)}, f32[32,256]{1,0:T(8,128)}, u32[]{:S(2)}) copy-start(f32[32,256]{1,0:T(8,128)} %inverse_ref.1) | copy-start | bytes 98308
  15.5 7.6 %collective-permute-start.8 = (bf16[256,256]{1,0:T(8,128)(2,1)S(1)}, bf16[256,256]{1,0:T(8,128)(2,1)S(1)}, u32[]{:S(2)}, u32[]{:S(2)}) collective-permute-start(bf16[256,256]{1,0:T(8,128)(2,1)S(1)} %after.1), channel_id=1, source_target_pairs={{0,6},{1,7},{2,4},{3,5},{4,2},{5,3},{6,0},{7,1},{8,14},{9,15},{10,... | collective-permute-start | bytes 393224 | tf_op jit(solution)/shard_map/ppermute | solution.py:24
  17.7 6.7 %collective-permute-start.9 = (bf16[512,256]{1,0:T(8,128)(2,1)S(1)}, bf16[512,256]{1,0:T(8,128)(2,1)S(1)}, u32[]{:S(2)}, u32[]{:S(2)}) collective-permute-start(bf16[512,256]{1,0:T(8,128)(2,1)S(1)} %collective-permute-done.3.refs_4_), channel_id=1, source_target_pairs={{0,1},{1,0},{2,3},{3,2},{4,5},{5,4},{6,7},{7,6},{8,9},{9,8},{10,11... | collective-permute-start | bytes 786440 | tf_op jit(solution)/shard_map/ppermute | solution.py:24
  17.7 5.6 %collective-permute-start.4 = (bf16[256,256]{1,0:T(8,128)(2,1)S(1)}, bf16[256,256]{1,0:T(8,128)(2,1)S(1)}, u32[]{:S(2)}, u32[]{:S(2)}) collective-permute-start(bf16[256,256]{1,0:T(8,128)(2,1)S(1)} %collective-permute-done.2.high_ref.refs_3_), channel_id=1, source_target_pairs={{0,1},{1,0},{2,3},{3,2},{4,5},{5,4},{6,7},{7,6},{8,9},{9,8},{10,11... | collective-permute-start | bytes 393224 | tf_op jit(solution)/shard_map/ppermute | solution.py:24
  20.5 2.9 %collective-permute-start.11 = (bf16[256,256]{1,0:T(8,128)(2,1)S(1)}, bf16[256,256]{1,0:T(8,128)(2,1)S(1)}, u32[]{:S(2)}, u32[]{:S(2)}) collective-permute-start(bf16[256,256]{1,0:T(8,128)(2,1)S(1)} %collective-permute-done.7.refs_8_), channel_id=1, source_target_pairs={{0,1},{1,0},{2,3},{3,2},{4,5},{5,4},{6,7},{7,6},{8,9},{9,8},{10,11... | collective-permute-start | bytes 393224 | tf_op jit(solution)/shard_map/ppermute | solution.py:24
  20.5 2.8 %collective-permute-start.10 = (bf16[256,256]{1,0:T(8,128)(2,1)S(1)}, bf16[256,256]{1,0:T(8,128)(2,1)S(1)}, u32[]{:S(2)}, u32[]{:S(2)}) collective-permute-start(bf16[256,256]{1,0:T(8,128)(2,1)S(1)} %collective-permute-done.6.refs_7_), channel_id=1, source_target_pairs={{0,1},{1,0},{2,3},{3,2},{4,5},{5,4},{6,7},{7,6},{8,9},{9,8},{10,11... | collective-permute-start | bytes 393224 | tf_op jit(solution)/shard_map/ppermute | solution.py:24
  23.1 1.3 %collective-permute-start.12 = (bf16[256,256]{1,0:T(8,128)(2,1)S(1)}, bf16[256,256]{1,0:T(8,128)(2,1)S(1)}, u32[]{:S(2)}, u32[]{:S(2)}) collective-permute-start(bf16[256,256]{1,0:T(8,128)(2,1)S(1)} %collective-permute-done.8.refs_9_), channel_id=1, source_target_pairs={{0,1},{1,0},{2,3},{3,2},{4,5},{5,4},{6,7},{7,6},{8,9},{9,8},{10,11... | collective-permute-start | bytes 393224 | tf_op jit(solution)/shard_map/ppermute | solution.py:24
  25.5 1.4 %collective-permute-start.13 = (f32[128,256]{1,0:T(8,128)S(1)}, f32[128,256]{1,0:T(8,128)S(1)}, u32[]{:S(2)}, u32[]{:S(2)}) collective-permute-start(f32[128,256]{1,0:T(8,128)S(1)} %get-tuple-element.14), channel_id=1, source_target_pairs={{0,1},{1,0},{2,3},{3,2},{4,5},{5,4},{6,7},{7,6},{8,9},{9,8},{10,11... | collective-permute-start | bytes 393224 | tf_op jit(solution)/shard_map/ppermute | solution.py:24
  26.9 5.0 %collective-permute-start.14 = (f32[64,256]{1,0:T(8,128)S(1)}, f32[64,256]{1,0:T(8,128)S(1)}, u32[]{:S(2)}, u32[]{:S(2)}) collective-permute-start(f32[64,256]{1,0:T(8,128)S(1)} %get-tuple-element.17), channel_id=1, source_target_pairs={{0,2},{1,5},{2,0},{3,7},{4,6},{5,1},{6,4},{7,3},{8,10},{9,13},{10,... | collective-permute-start | bytes 196616 | tf_op jit(solution)/shard_map/ppermute | solution.py:24
  29.3 4.5 %collective-permute-start.15 = (f32[64,256]{1,0:T(8,128)S(1)}, f32[64,256]{1,0:T(8,128)S(1)}, u32[]{:S(2)}, u32[]{:S(2)}) collective-permute-start(f32[64,256]{1,0:T(8,128)S(1)} %get-tuple-element.18), channel_id=1, source_target_pairs={{0,4},{1,3},{2,6},{3,1},{4,0},{5,7},{6,2},{7,5},{8,12},{9,11},{10,... | collective-permute-start | bytes 196616 | tf_op jit(solution)/shard_map/ppermute | solution.py:24
  29.4 5.2 %collective-permute-start.16 = (f32[64,256]{1,0:T(8,128)S(1)}, f32[64,256]{1,0:T(8,128)S(1)}, u32[]{:S(2)}, u32[]{:S(2)}) collective-permute-start(f32[64,256]{1,0:T(8,128)S(1)} %get-tuple-element.19), channel_id=1, source_target_pairs={{0,6},{1,7},{2,4},{3,5},{4,2},{5,3},{6,0},{7,1},{8,14},{9,15},{10,... | collective-permute-start | bytes 196616 | tf_op jit(solution)/shard_map/ppermute | solution.py:24
  34.6 4.9 %collective-permute-start.17 = (f32[32,256]{1,0:T(8,128)S(1)}, f32[32,256]{1,0:T(8,128)S(1)}, u32[]{:S(2)}, u32[]{:S(2)}) collective-permute-start(f32[32,256]{1,0:T(8,128)S(1)} %get-tuple-element.21), channel_id=1, source_target_pairs={{0,8},{1,9},{2,10},{3,11},{4,12},{5,13},{6,14},{7,15},{8,0},{9,1},... | collective-permute-start | bytes 98312 | tf_op jit(solution)/shard_map/ppermute | solution.py:24

commit v3 on v2

v3 whole, which is shorter than its diff:
```python
import functools

import jax
import jax.numpy as jnp
from jax import lax
from jax.experimental import pallas as pl
from jax.experimental.pallas import tpu as pltpu
from jax.sharding import PartitionSpec as P

NCH = 2
CW = 256
MIB = 2**20
QUAD = ((0, 0), (1, 2), (2, 1), (3, 3))
SMEM = pl.BlockSpec(memory_space=pltpu.SMEM)
VMEM = pl.BlockSpec(memory_space=pltpu.VMEM)
ANY = pl.BlockSpec(memory_space=pl.ANY)
TOKEN = pltpu.VMEM((8, 128), jnp.float32)


def params(mib):
    return pltpu.CompilerParams(vmem_limit_bytes=mib * MIB)


def exchange(block, n, masks):
    return lax.ppermute(block, "row", [(i, i ^ masks[i % 2]) for i in range(n)])


def compact_kernel(coupling_ref, panel_ref, block_ref):
    child = coupling_ref[lax.axis_index("row")]
    start = pl.multiple_of(jnp.minimum(child, NCH - 1) * CW, CW)
    block_ref[...] = panel_ref[:, pl.ds(start, CW)]


def load_kernel(mine_hbm, other_hbm, mine_ref, other_ref, sems):
    rows = mine_hbm.shape[0]
    core = lax.rem(lax.axis_index("row"), 2)
    copies = []
    for pair in range(mine_ref.shape[1] // rows):
        here = pl.ds(pl.multiple_of((2 * pair + core) * rows, rows), rows)
        there = pl.ds(pair * rows, rows)
        for number, (source, ref) in enumerate(
            ((mine_hbm, mine_ref), (other_hbm, other_ref))
        ):
            copies.append(
                pltpu.make_async_copy(
                    source.at[:, here], ref.at[:, there], sems.at[pair, number]
                )
            )
    for copy in copies:
        copy.start()
    for copy in copies:
        copy.wait()


def after_kernel(block_ref, after_ref, out_ref):
    out_ref[...] = block_ref[...]


def join_kernel(low_ref, high_ref, after_ref, out_ref):
    rows = low_ref.shape[0]
    out_ref[:rows] = low_ref[...]
    out_ref[rows:] = high_ref[...]


def product_kernel(n, places, coupling_ref, mine_z, other_z, other_own, *refs):
    block_refs = refs[:-4]
    mine_ref, other_ref, send_ref, keep_ref = refs[-4:]
    rows = mine_z.shape[0]
    me = lax.axis_index("row")
    core = lax.rem(me, 2)
    children = (coupling_ref[me], coupling_ref[me ^ 1])
    for total_ref in (mine_ref, other_ref):
        total_ref[...] = jnp.zeros_like(total_ref)
    for held, block_ref in zip(places, block_refs):
        for number, (even, odd) in enumerate(held):
            tile = me ^ jnp.where(core == 0, even, odd)
            tile_child = coupling_ref[tile]
            columns = pl.ds(pl.multiple_of(lax.div(tile, 2) * rows, rows), rows)
            for child, z_ref, total_ref in zip(
                children, (mine_z, other_z), (mine_ref, other_ref)
            ):

                @pl.when((tile_child == child) & (child < NCH))
                def _():
                    total_ref[...] += jnp.dot(
                        z_ref[:, columns],
                        block_ref[number * rows:(number + 1) * rows],
                        preferred_element_type=jnp.float32,
                    )

    terms = []
    for left_ref, total_ref in ((block_refs[0], mine_ref), (other_own, other_ref)):
        total = total_ref[...]
        high = total.astype(jnp.bfloat16)
        low = (total - high.astype(jnp.float32)).astype(jnp.bfloat16)
        left = left_ref[...]
        terms.append(
            sum(
                lax.dot_general(
                    left, part, (((0,), (0,)), ((), ())), preferred_element_type=jnp.float32
                )
                for part in (high, low)
            )
        )
    piece = NCH * CW // n
    zero = jnp.zeros((piece, CW), jnp.float32)
    for child in range(NCH):
        for q in range(CW // piece // 2):
            low, high = [
                sum(
                    jnp.where(mine == child, term[at:at + piece], zero)
                    for mine, term in zip(children, terms)
                )
                for at in (2 * q * piece, (2 * q + 1) * piece)
            ]
            at = child * (CW // 2) + q * piece
            keep_ref[at:at + piece] = jnp.where(core == 0, low, high)
            send_ref[at:at + piece] = jnp.where(core == 0, high, low)


def offdiag_kernel(coupling_ref, mine_ref, other_ref, offdiag_ref, token_ref):
    token_ref[...] = jnp.zeros_like(token_ref)
    child = coupling_ref[lax.axis_index("row")]
    product = mine_ref[...] + other_ref[...]
    for k in range(NCH):
        offdiag_ref[:, k * CW:(k + 1) * CW] = jnp.where(
            child == k, -product, jnp.zeros_like(product)
        )


def quad_kernel(piece, kept_ref, got_ref, *out_refs):
    me = lax.axis_index("row")
    core = lax.rem(me, 2)
    low = lax.rem(lax.div(me, 2), 4)
    for (even, odd), out_ref in zip(QUAD, out_refs):
        want = low ^ jnp.where(core == 0, even, odd)
        for group in range(out_ref.shape[0] // piece):
            rows = pl.ds(pl.multiple_of((group * 4 + want) * piece, piece), piece)
            out_ref[group * piece:(group + 1) * piece] = kept_ref[rows] + got_ref[rows]


def halve_kernel(piece, bit, *refs):
    part_refs, send_ref, keep_ref = refs[:-2], refs[-2], refs[-1]
    mine = lax.rem(lax.div(lax.axis_index("row"), 2 << bit), 2)
    for out_ref, side in ((keep_ref, mine), (send_ref, 1 - mine)):
        for index in range(out_ref.shape[0] // piece):
            rows = pl.ds(pl.multiple_of((2 * index + side) * piece, piece), piece)
            total = part_refs[0][rows]
            for part_ref in part_refs[1:]:
                total = total + part_ref[rows]
            out_ref[index * piece:(index + 1) * piece] = total


def last_kernel(inverse_ref, kept_ref, got_ref, after_ref, diag_ref):
    diag_ref[...] = inverse_ref[...] + (kept_ref[...] + got_ref[...])


def after(block, other):
    return pl.pallas_call(
        after_kernel,
        out_shape=pltpu.VMEM(block.shape, block.dtype),
        in_specs=[VMEM, ANY],
        out_specs=VMEM,
        compiler_params=params(2),
        name="after",
    )(block, other)


def gather(block, inverse_root, n):
    rows = block.shape[0]
    held = {"own": ([(0, 0)], block)}

    def fetch(name, source, masks):
        tiles, held_block = held[source]
        held[name] = (
            [tuple(masks[c] ^ pair[c] for c in range(2)) for pair in tiles],
            exchange(held_block, n, masks),
        )

    fetch("d", "own", (8, 8))
    other_own = exchange(block, n, (1, 1))
    fetch("a", "own", (2, 4))
    other_z = exchange(lax.optimization_barrier((inverse_root, block))[0], n, (1, 1))
    half = pltpu.VMEM((rows, inverse_root.shape[1] // 2), inverse_root.dtype)
    mine_z, other_z = pl.pallas_call(
        load_kernel,
        out_shape=[half, half],
        in_specs=[ANY, ANY],
        out_specs=[VMEM] * 2,
        scratch_shapes=[pltpu.SemaphoreType.DMA((n // 2, 2))],
        compiler_params=params(62 - inverse_root.size * 2 // MIB),
        name="load",
    )(inverse_root, other_z)
    pair = pl.pallas_call(
        join_kernel,
        out_shape=pltpu.VMEM((2 * rows, CW), block.dtype),
        in_specs=[VMEM, VMEM, ANY],
        out_specs=VMEM,
        compiler_params=params(2),
        name="join",
    )(block, held["a"][1], mine_z)
    held["pair"] = (held["own"][0] + held["a"][0], pair)
    fetch("bc", "pair", (4, 2))
    del held["pair"]
    fetch("g", "d", (6, 6))
    fetch("f", "d", (2, 4))
    fetch("e", "d", (4, 2))
    for bit in range(4, n.bit_length() - 1):
        for name in list(held):
            fetch(f"{name}_{bit}", name, (1 << bit, 1 << bit))
    return mine_z, other_z, other_own, list(held.values())


def per_device(n, inverse_root, lower_panel, coupling, child_inverse):
    rows = inverse_root.shape[0]
    block = pl.pallas_call(
        compact_kernel,
        out_shape=pltpu.VMEM((rows, CW), lower_panel.dtype),
        in_specs=[SMEM, VMEM],
        out_specs=VMEM,
        compiler_params=params(60),
        name="compact",
    )(coupling, lower_panel)
    mine_z, other_z, other_own, held = gather(block, inverse_root, n)
    mine, other, send, keep = pl.pallas_call(
        functools.partial(product_kernel, n, [places for places, _ in held]),
        out_shape=[
            jax.ShapeDtypeStruct((rows, CW), jnp.float32),
            jax.ShapeDtypeStruct((rows, CW), jnp.float32),
            jax.ShapeDtypeStruct((NCH * CW // 2, CW), jnp.float32),
            jax.ShapeDtypeStruct((NCH * CW // 2, CW), jnp.float32),
        ],
        in_specs=[SMEM] + [VMEM] * (len(held) + 3),
        out_specs=[VMEM] * 4,
        compiler_params=params(24 if n > 16 else 8),
        name="product",
    )(coupling, mine_z, other_z, other_own, *[block for _, block in held])
    got = exchange(send, n, (1, 1))
    piece = NCH * CW // n
    width = NCH * CW // 2 // len(QUAD)
    parts = list(pl.pallas_call(
        functools.partial(quad_kernel, piece),
        out_shape=[jax.ShapeDtypeStruct((width, CW), jnp.float32)] * len(QUAD),
        in_specs=[VMEM] * 2,
        out_specs=[VMEM] * len(QUAD),
        compiler_params=params(2),
        name="quad",
    )(keep, got))
    offdiag, token = pl.pallas_call(
        offdiag_kernel,
        out_shape=[jax.ShapeDtypeStruct((rows, NCH * CW), jnp.float32), TOKEN],
        in_specs=[SMEM, VMEM, VMEM],
        out_specs=[VMEM] * 2,
        compiler_params=params(4),
        name="offdiag",
    )(coupling, mine, exchange(after(other, parts[0]), n, (1, 1)))
    for number in range(1, len(QUAD)):
        parts[number] = exchange(parts[number], n, tuple(2 * m for m in QUAD[number]))
    for bit in range(2, (n // 2).bit_length() - 1):
        width //= 2
        send, keep = pl.pallas_call(
            functools.partial(halve_kernel, piece, bit),
            out_shape=[jax.ShapeDtypeStruct((width, CW), jnp.float32)] * 2,
            in_specs=[VMEM] * len(parts),
            out_specs=[VMEM] * 2,
            compiler_params=params(2),
            name=f"halve{bit}",
        )(*parts)
        got = exchange(send, n, (2 << bit, 2 << bit))
        parts = [keep, got]
    child_diag = pl.pallas_call(
        last_kernel,
        out_shape=jax.ShapeDtypeStruct((piece, CW), jnp.float32),
        in_specs=[VMEM] * 4,
        out_specs=VMEM,
        compiler_params=params(2),
        name="last",
    )(child_inverse, keep, got, token)
    return offdiag, child_diag


def solution(mesh):
    split = P(("pole", "row"), None)
    return jax.shard_map(
        functools.partial(per_device, mesh.shape["row"]),
        mesh=mesh,
        in_specs=(split, split, P(), split),
        out_specs=(split, split),
        check_vma=False,
    )
```

time: 40.4 us -> 39.1 us (0.968); the launches traced: 40.1 us -> 39.2 us
  starting transfers between devices: 19 us -> 16.6 us
  waiting for transfers between devices: 14 us -> 15.2 us
  Pallas kernels: 5.67 us -> 6.62 us
  local copies, waits for them, and re-layouts: 0.67 us -> 0.01 us
    ppermute x18 -> x14, starting transfers between devices: 19 us -> 16.6 us  [exchange(): return lax.ppermute(block, 'row', [(i, i ^ masks[i % 2]) for i in range(n)])]
    ppermute x18 -> x14, waiting for transfers between devices: 14 us -> 15.2 us  [exchange(): return lax.ppermute(block, 'row', [(i, i ^ masks[i % 2]) for i in range(n)])]
    pallas_call x4, Pallas kernels: 4 us -> 4.95 us  [the longest x1 1.77 us: per_device(): pl.pallas_call(functools.partial(product_kernel, n, [places for places, _...]
    unnamed x8 -> x4, local copies, waits for them, and re-layouts: 0.67 us -> 0.01 us
  transfers between devices with their start and end apart: 18 -> 14, of which waited for: 10 -> 8; matrix products, arithmetic and copies ran while one was open for 0% -> 0% of each run, Pallas kernels for 8% -> 8%
where the time goes in v3:
time: 39.1 us; the launch traced here: 39.2 us
  starting transfers between devices  16.6 us (42%)
  waiting for transfers between devices  15.2 us (39%)
  Pallas kernels  6.62 us (17%)
  between operations  0.73 us (2%)
    ppermute x14, starting transfers between devices, exchange(): return lax.ppermute(block, 'row', [(i, i ^ masks[i % 2]) for i in range(n)])  16.6 us
    ppermute x14, waiting for transfers between devices, exchange(): return lax.ppermute(block, 'row', [(i, i ^ masks[i % 2]) for i in range(n)])  15.2 us
    pallas_call x1, Pallas kernels, per_device(): pl.pallas_call(functools.partial(product_kernel, n, [places for places, _...  1.77 us
    pallas_call x1, Pallas kernels, gather(): pl.pallas_call(load_kernel, out_shape=[half, half], in_specs=[ANY, ANY],...  1.77 us
    pallas_call x1, Pallas kernels, per_device(): pl.pallas_call(offdiag_kernel, out_shape=[jax.ShapeDtypeStruct((rows, NCH...  1.39 us
    pallas_call x1, Pallas kernels, per_device(): pl.pallas_call(compact_kernel, out_shape=pltpu.VMEM((rows, CW), lower_pan...  0.98 us
  transfers between devices with their start and end apart: 14, of which 8 were waited for; matrix products, arithmetic and copies ran while one was open for 0% of the time, Pallas kernels for 8%

profile of v3, /device:TPU:0, one launch (start us, length us, event | category | flops | bytes accessed | tf_op | source)
XLA Modules:
  0.0 39.2 jit_solution(14200696112226873229)
XLA Ops:
  0.6 1.0 %compact.1.low_ref.refs_0_ = bf16[256,256]{1,0:T(8,128)(2,1)S(1)} custom-call(s32[16]{0:T(128)} %coupling_ref.5, bf16[256,512]{1,0:T(8,128)(2,1)} %panel_ref.1), custom_call_target="tpu_custom_call" | custom-call | tf_op jit(solution)/shard_map/compact/pallas_call | solution.py:216
  1.6 0.0 copy-start.1
  1.6 0.5 %collective-permute-start = (bf16[256,4096]{1,0:T(8,128)(2,1)}, bf16[256,4096]{1,0:T(8,128)(2,1)}, u32[]{:S(2)}, u32[]{:S(2)}) collective-permute-start(bf16[256,4096]{1,0:T(8,128)(2,1)} %mine_hbm.1), channel_id=1, source_target_pairs={{0,1},{1,0},{2,3},{3,2},{4,5},{5,4},{6,7},{7,6},{8,9},{9,8},{10,11... | collective-permute-start | bytes 6291464 | tf_op jit(solution)/shard_map/ppermute | solution.py:25
  2.2 2.6 %collective-permute-start.3 = (bf16[256,256]{1,0:T(8,128)(2,1)S(1)}, bf16[256,256]{1,0:T(8,128)(2,1)S(1)}, u32[]{:S(2)}, u32[]{:S(2)}) collective-permute-start(bf16[256,256]{1,0:T(8,128)(2,1)S(1)} %compact.1.low_ref.refs_0_), channel_id=1, source_target_pairs={{0,2},{1,5},{2,0},{3,7},{4,6},{5,1},{6,4},{7,3},{8,10},{9,13},{10,... | collective-permute-start | bytes 393224 | tf_op jit(solution)/shard_map/ppermute | solution.py:25
  4.7 2.6 %collective-permute-start.2 = (bf16[256,256]{1,0:T(8,128)(2,1)S(1)}, bf16[256,256]{1,0:T(8,128)(2,1)S(1)}, u32[]{:S(2)}, u32[]{:S(2)}) collective-permute-start(bf16[256,256]{1,0:T(8,128)(2,1)S(1)} %compact.1.low_ref.refs_0_), channel_id=1, source_target_pairs={{0,8},{1,9},{2,10},{3,11},{4,12},{5,13},{6,14},{7,15},{8,0},{9,1},... | collective-permute-start | bytes 393224 | tf_op jit(solution)/shard_map/ppermute | solution.py:25
  7.3 0.0 collective-permute-done.other_hbm
  7.3 1.8 %load.1 = (bf16[256,2048]{1,0:T(8,128)(2,1)S(1)}, bf16[256,2048]{1,0:T(8,128)(2,1)S(1)}) custom-call(bf16[256,4096]{1,0:T(8,128)(2,1)} %mine_hbm.1, bf16[256,4096]{1,0:T(8,128)(2,1)} %collective-permute-done.other_hbm), custom_call_target="tpu_custom_call" | custom-call | tf_op jit(solution)/shard_map/load/pallas_call | solution.py:185
  9.1 0.0 collective-permute-done.3.high_ref.refs_2_
  9.2 1.9 %collective-permute-start.4 = (bf16[512,256]{1,0:T(8,128)(2,1)S(1)}, bf16[512,256]{1,0:T(8,128)(2,1)S(1)}, u32[]{:S(2)}, u32[]{:S(2)}) collective-permute-start(bf16[512,256]{1,0:T(8,128)(2,1)S(1)} %join.1), channel_id=1, source_target_pairs={{0,4},{1,3},{2,6},{3,1},{4,0},{5,7},{6,2},{7,5},{8,12},{9,11},{10,... | collective-permute-start | bytes 786440 | tf_op jit(solution)/shard_map/ppermute | solution.py:25
  11.1 0.0 collective-permute-start.1
  11.1 3.1 %collective-permute-done.2.refs_1_ = bf16[256,256]{1,0:T(8,128)(2,1)S(1)} collective-permute-done((bf16[256,256]{1,0:T(8,128)(2,1)S(1)}, bf16[256,256]{1,0:T(8,128)(2,1)S(1)}, u32[]{:S(2)}, u32[]{:S(2)}) %collective-permute-start.2) | collective-permute-done | bytes 131104 | tf_op jit(solution)/shard_map/ppermute | solution.py:25
  14.2 0.5 %collective-permute-start.5 = (bf16[256,256]{1,0:T(8,128)(2,1)S(1)}, bf16[256,256]{1,0:T(8,128)(2,1)S(1)}, u32[]{:S(2)}, u32[]{:S(2)}) collective-permute-start(bf16[256,256]{1,0:T(8,128)(2,1)S(1)} %collective-permute-done.2.refs_1_), channel_id=1, source_target_pairs={{0,6},{1,7},{2,4},{3,5},{4,2},{5,3},{6,0},{7,1},{8,14},{9,15},{10,... | collective-permute-start | bytes 393224 | tf_op jit(solution)/shard_map/ppermute | solution.py:25
  14.7 0.6 %collective-permute-start.6 = (bf16[256,256]{1,0:T(8,128)(2,1)S(1)}, bf16[256,256]{1,0:T(8,128)(2,1)S(1)}, u32[]{:S(2)}, u32[]{:S(2)}) collective-permute-start(bf16[256,256]{1,0:T(8,128)(2,1)S(1)} %collective-permute-done.2.refs_1_), channel_id=1, source_target_pairs={{0,2},{1,5},{2,0},{3,7},{4,6},{5,1},{6,4},{7,3},{8,10},{9,13},{10,... | collective-permute-start | bytes 393224 | tf_op jit(solution)/shard_map/ppermute | solution.py:25
  15.2 2.4 %collective-permute-start.7 = (bf16[256,256]{1,0:T(8,128)(2,1)S(1)}, bf16[256,256]{1,0:T(8,128)(2,1)S(1)}, u32[]{:S(2)}, u32[]{:S(2)}) collective-permute-start(bf16[256,256]{1,0:T(8,128)(2,1)S(1)} %collective-permute-done.2.refs_1_), channel_id=1, source_target_pairs={{0,4},{1,3},{2,6},{3,1},{4,0},{5,7},{6,2},{7,5},{8,12},{9,11},{10,... | collective-permute-start | bytes 393224 | tf_op jit(solution)/shard_map/ppermute | solution.py:25
  17.7 0.0 collective-permute-done.1.other_own
  17.7 3.8 %collective-permute-done.5.refs_4_ = bf16[256,256]{1,0:T(8,128)(2,1)S(1)} collective-permute-done((bf16[256,256]{1,0:T(8,128)(2,1)S(1)}, bf16[256,256]{1,0:T(8,128)(2,1)S(1)}, u32[]{:S(2)}, u32[]{:S(2)}) %collective-permute-start.5) | collective-permute-done | bytes 131104 | tf_op jit(solution)/shard_map/ppermute | solution.py:25
  21.5 1.4 %collective-permute-done.6.refs_5_ = bf16[256,256]{1,0:T(8,128)(2,1)S(1)} collective-permute-done((bf16[256,256]{1,0:T(8,128)(2,1)S(1)}, bf16[256,256]{1,0:T(8,128)(2,1)S(1)}, u32[]{:S(2)}, u32[]{:S(2)}) %collective-permute-start.6) | collective-permute-done | bytes 131104 | tf_op jit(solution)/shard_map/ppermute | solution.py:25
  22.9 0.0 collective-permute-done.7.refs_6_
  22.9 0.0 collective-permute-done.4.refs_3_
  22.9 0.0 copy-done.1
  22.9 0.0 copy-start
  22.9 1.8 %product.1 = (f32[256,256]{1,0:T(8,128)S(1)}, f32[256,256]{1,0:T(8,128)S(1)}, f32[256,256]{1,0:T(8,128)S(1)}, f32[256,256]{1,0:T(8,128)S(1)}) custom-call(s32[16]{0:T(128)S(1)} %copy-done.1, bf16[256,2048]{1,0:T(8,128)(2,1)S(1)} %get-tuple-element.18.after_ref.mine_z, bf16[256,2048]{1,0:T(8,128)(2,1)S(1)} %get-tuple-element.19.other_z, ...), custom_call_target="tpu_custom_call" | custom-call | tf_op jit(solution)/shard_map/product/pallas_call | solution.py:225
  24.7 0.1 collective-permute-start.8
  24.7 1.5 %collective-permute-done.8.got_ref = f32[256,256]{1,0:T(8,128)S(1)} collective-permute-done((f32[256,256]{1,0:T(8,128)S(1)}, f32[256,256]{1,0:T(8,128)S(1)}, u32[]{:S(2)}, u32[]{:S(2)}) %collective-permute-start.8) | collective-permute-done | bytes 262176 | tf_op jit(solution)/shard_map/ppermute | solution.py:25
  26.3 0.2 collective-permute-start.9
  26.5 1.8 %collective-permute-start.10 = (f32[64,256]{1,0:T(8,128)S(1)}, f32[64,256]{1,0:T(8,128)S(1)}, u32[]{:S(2)}, u32[]{:S(2)}) collective-permute-start(f32[64,256]{1,0:T(8,128)S(1)} %get-tuple-element.26), channel_id=1, source_target_pairs={{0,2},{1,5},{2,0},{3,7},{4,6},{5,1},{6,4},{7,3},{8,10},{9,13},{10,... | collective-permute-start | bytes 196616 | tf_op jit(solution)/shard_map/ppermute | solution.py:25
  28.4 0.0 collective-permute-start.11
  28.4 1.7 %collective-permute-start.12 = (f32[64,256]{1,0:T(8,128)S(1)}, f32[64,256]{1,0:T(8,128)S(1)}, u32[]{:S(2)}, u32[]{:S(2)}) collective-permute-start(f32[64,256]{1,0:T(8,128)S(1)} %get-tuple-element.28), channel_id=1, source_target_pairs={{0,6},{1,7},{2,4},{3,5},{4,2},{5,3},{6,0},{7,1},{8,14},{9,15},{10,... | collective-permute-start | bytes 196616 | tf_op jit(solution)/shard_map/ppermute | solution.py:25
  30.0 1.3 %collective-permute-done.10.refs_1_ = f32[64,256]{1,0:T(8,128)S(1)} collective-permute-done((f32[64,256]{1,0:T(8,128)S(1)}, f32[64,256]{1,0:T(8,128)S(1)}, u32[]{:S(2)}, u32[]{:S(2)}) %collective-permute-start.10) | collective-permute-done | bytes 65568 | tf_op jit(solution)/shard_map/ppermute | solution.py:25
  31.3 1.3 %collective-permute-done.11.refs_2_ = f32[64,256]{1,0:T(8,128)S(1)} collective-permute-done((f32[64,256]{1,0:T(8,128)S(1)}, f32[64,256]{1,0:T(8,128)S(1)}, u32[]{:S(2)}, u32[]{:S(2)}) %collective-permute-start.11) | collective-permute-done | bytes 65568 | tf_op jit(solution)/shard_map/ppermute | solution.py:25
  32.6 1.0 %collective-permute-done.12.refs_3_ = f32[64,256]{1,0:T(8,128)S(1)} collective-permute-done((f32[64,256]{1,0:T(8,128)S(1)}, f32[64,256]{1,0:T(8,128)S(1)}, u32[]{:S(2)}, u32[]{:S(2)}) %collective-permute-start.12) | collective-permute-done | bytes 65568 | tf_op jit(solution)/shard_map/ppermute | solution.py:25
  33.7 1.7 %collective-permute-start.13 = (f32[32,256]{1,0:T(8,128)S(1)}, f32[32,256]{1,0:T(8,128)S(1)}, u32[]{:S(2)}, u32[]{:S(2)}) collective-permute-start(f32[32,256]{1,0:T(8,128)S(1)} %get-tuple-element.30), channel_id=1, source_target_pairs={{0,8},{1,9},{2,10},{3,11},{4,12},{5,13},{6,14},{7,15},{8,0},{9,1},... | collective-permute-start | bytes 98312 | tf_op jit(solution)/shard_map/ppermute | solution.py:25
  35.4 0.0 collective-permute-done.9.other_ref
  35.4 1.4 %offdiag.1 = (f32[256,512]{1,0:T(8,128)}, f32[8,128]{1,0:T(8,128)S(1)}) custom-call(s32[16]{0:T(128)S(1)} %copy-done.1, f32[256,256]{1,0:T(8,128)S(1)} %get-tuple-element.20.mine_ref, f32[256,256]{1,0:T(8,128)S(1)} %collective-permute-done.9.other_ref), custom_call_target="tpu_custom_call" | custom-call | tf_op jit(solution)/shard_map/offdiag/pallas_call | solution.py:249
  36.8 1.8 %collective-permute-done.13.got_ref = f32[32,256]{1,0:T(8,128)S(1)} collective-permute-done((f32[32,256]{1,0:T(8,128)S(1)}, f32[32,256]{1,0:T(8,128)S(1)}, u32[]{:S(2)}, u32[]{:S(2)}) %collective-permute-start.13) | collective-permute-done | bytes 32800 | tf_op jit(solution)/shard_map/ppermute | solution.py:25
  38.6 0.0 copy-done
  38.6 0.6 %last.1 = f32[32,256]{1,0:T(8,128)} custom-call(f32[32,256]{1,0:T(8,128)S(1)} %copy-done, f32[32,256]{1,0:T(8,128)S(1)} %get-tuple-element.29.kept_ref, f32[32,256]{1,0:T(8,128)S(1)} %collective-permute-done.13.got_ref, f32[8,128]{1,0:T(8,128)S(1)} %get-tuple-element.31.after_ref), custom_call_target="tpu_custom_call" | custom-call | tf_op jit(solution)/shard_map/last/pallas_call | solution.py:271
  (4 shorter events, 0.1 us)
Async XLA Ops:
  1.6 21.2 %copy-start.1 = (s32[16]{0:T(128)S(1)}, s32[16]{0:T(128)}, u32[]{:S(2)}) copy-start(s32[16]{0:T(128)} %coupling_ref.5) | copy-start | bytes 196
  1.6 5.7 %collective-permute-start = (bf16[256,4096]{1,0:T(8,128)(2,1)}, bf16[256,4096]{1,0:T(8,128)(2,1)}, u32[]{:S(2)}, u32[]{:S(2)}) collective-permute-start(bf16[256,4096]{1,0:T(8,128)(2,1)} %mine_hbm.1), channel_id=1, source_target_pairs={{0,1},{1,0},{2,3},{3,2},{4,5},{5,4},{6,7},{7,6},{8,9},{9,8},{10,11... | collective-permute-start | bytes 6291464 | tf_op jit(solution)/shard_map/ppermute | solution.py:25
  2.2 7.0 %collective-permute-start.3 = (bf16[256,256]{1,0:T(8,128)(2,1)S(1)}, bf16[256,256]{1,0:T(8,128)(2,1)S(1)}, u32[]{:S(2)}, u32[]{:S(2)}) collective-permute-start(bf16[256,256]{1,0:T(8,128)(2,1)S(1)} %compact.1.low_ref.refs_0_), channel_id=1, source_target_pairs={{0,2},{1,5},{2,0},{3,7},{4,6},{5,1},{6,4},{7,3},{8,10},{9,13},{10,... | collective-permute-start | bytes 393224 | tf_op jit(solution)/shard_map/ppermute | solution.py:25
  4.7 9.4 %collective-permute-start.2 = (bf16[256,256]{1,0:T(8,128)(2,1)S(1)}, bf16[256,256]{1,0:T(8,128)(2,1)S(1)}, u32[]{:S(2)}, u32[]{:S(2)}) collective-permute-start(bf16[256,256]{1,0:T(8,128)(2,1)S(1)} %compact.1.low_ref.refs_0_), channel_id=1, source_target_pairs={{0,8},{1,9},{2,10},{3,11},{4,12},{5,13},{6,14},{7,15},{8,0},{9,1},... | collective-permute-start | bytes 393224 | tf_op jit(solution)/shard_map/ppermute | solution.py:25
  9.2 13.7 %collective-permute-start.4 = (bf16[512,256]{1,0:T(8,128)(2,1)S(1)}, bf16[512,256]{1,0:T(8,128)(2,1)S(1)}, u32[]{:S(2)}, u32[]{:S(2)}) collective-permute-start(bf16[512,256]{1,0:T(8,128)(2,1)S(1)} %join.1), channel_id=1, source_target_pairs={{0,4},{1,3},{2,6},{3,1},{4,0},{5,7},{6,2},{7,5},{8,12},{9,11},{10,... | collective-permute-start | bytes 786440 | tf_op jit(solution)/shard_map/ppermute | solution.py:25
  11.1 6.6 %collective-permute-start.1 = (bf16[256,256]{1,0:T(8,128)(2,1)S(1)}, bf16[256,256]{1,0:T(8,128)(2,1)S(1)}, u32[]{:S(2)}, u32[]{:S(2)}) collective-permute-start(bf16[256,256]{1,0:T(8,128)(2,1)S(1)} %compact.1.low_ref.refs_0_), channel_id=1, source_target_pairs={{0,1},{1,0},{2,3},{3,2},{4,5},{5,4},{6,7},{7,6},{8,9},{9,8},{10,11... | collective-permute-start | bytes 393224 | tf_op jit(solution)/shard_map/ppermute | solution.py:25
  14.2 7.3 %collective-permute-start.5 = (bf16[256,256]{1,0:T(8,128)(2,1)S(1)}, bf16[256,256]{1,0:T(8,128)(2,1)S(1)}, u32[]{:S(2)}, u32[]{:S(2)}) collective-permute-start(bf16[256,256]{1,0:T(8,128)(2,1)S(1)} %collective-permute-done.2.refs_1_), channel_id=1, source_target_pairs={{0,6},{1,7},{2,4},{3,5},{4,2},{5,3},{6,0},{7,1},{8,14},{9,15},{10,... | collective-permute-start | bytes 393224 | tf_op jit(solution)/shard_map/ppermute | solution.py:25
  14.7 8.2 %collective-permute-start.6 = (bf16[256,256]{1,0:T(8,128)(2,1)S(1)}, bf16[256,256]{1,0:T(8,128)(2,1)S(1)}, u32[]{:S(2)}, u32[]{:S(2)}) collective-permute-start(bf16[256,256]{1,0:T(8,128)(2,1)S(1)} %collective-permute-done.2.refs_1_), channel_id=1, source_target_pairs={{0,2},{1,5},{2,0},{3,7},{4,6},{5,1},{6,4},{7,3},{8,10},{9,13},{10,... | collective-permute-start | bytes 393224 | tf_op jit(solution)/shard_map/ppermute | solution.py:25
  15.2 7.6 %collective-permute-start.7 = (bf16[256,256]{1,0:T(8,128)(2,1)S(1)}, bf16[256,256]{1,0:T(8,128)(2,1)S(1)}, u32[]{:S(2)}, u32[]{:S(2)}) collective-permute-start(bf16[256,256]{1,0:T(8,128)(2,1)S(1)} %collective-permute-done.2.refs_1_), channel_id=1, source_target_pairs={{0,4},{1,3},{2,6},{3,1},{4,0},{5,7},{6,2},{7,5},{8,12},{9,11},{10,... | collective-permute-start | bytes 393224 | tf_op jit(solution)/shard_map/ppermute | solution.py:25
  22.9 15.7 %copy-start = (f32[32,256]{1,0:T(8,128)S(1)}, f32[32,256]{1,0:T(8,128)}, u32[]{:S(2)}) copy-start(f32[32,256]{1,0:T(8,128)} %inverse_ref.1) | copy-start | bytes 98308
  24.7 1.6 %collective-permute-start.8 = (f32[256,256]{1,0:T(8,128)S(1)}, f32[256,256]{1,0:T(8,128)S(1)}, u32[]{:S(2)}, u32[]{:S(2)}) collective-permute-start(f32[256,256]{1,0:T(8,128)S(1)} %get-tuple-element.23), channel_id=1, source_target_pairs={{0,1},{1,0},{2,3},{3,2},{4,5},{5,4},{6,7},{7,6},{8,9},{9,8},{10,11... | collective-permute-start | bytes 786440 | tf_op jit(solution)/shard_map/ppermute | solution.py:25
  26.3 9.1 %collective-permute-start.9 = (f32[256,256]{1,0:T(8,128)S(1)}, f32[256,256]{1,0:T(8,128)S(1)}, u32[]{:S(2)}, u32[]{:S(2)}) collective-permute-start(f32[256,256]{1,0:T(8,128)S(1)} %after.1), channel_id=1, source_target_pairs={{0,1},{1,0},{2,3},{3,2},{4,5},{5,4},{6,7},{7,6},{8,9},{9,8},{10,11... | collective-permute-start | bytes 786440 | tf_op jit(solution)/shard_map/ppermute | solution.py:25
  26.5 4.8 %collective-permute-start.10 = (f32[64,256]{1,0:T(8,128)S(1)}, f32[64,256]{1,0:T(8,128)S(1)}, u32[]{:S(2)}, u32[]{:S(2)}) collective-permute-start(f32[64,256]{1,0:T(8,128)S(1)} %get-tuple-element.26), channel_id=1, source_target_pairs={{0,2},{1,5},{2,0},{3,7},{4,6},{5,1},{6,4},{7,3},{8,10},{9,13},{10,... | collective-permute-start | bytes 196616 | tf_op jit(solution)/shard_map/ppermute | solution.py:25
  28.4 4.3 %collective-permute-start.11 = (f32[64,256]{1,0:T(8,128)S(1)}, f32[64,256]{1,0:T(8,128)S(1)}, u32[]{:S(2)}, u32[]{:S(2)}) collective-permute-start(f32[64,256]{1,0:T(8,128)S(1)} %get-tuple-element.27), channel_id=1, source_target_pairs={{0,4},{1,3},{2,6},{3,1},{4,0},{5,7},{6,2},{7,5},{8,12},{9,11},{10,... | collective-permute-start | bytes 196616 | tf_op jit(solution)/shard_map/ppermute | solution.py:25
  28.4 5.3 %collective-permute-start.12 = (f32[64,256]{1,0:T(8,128)S(1)}, f32[64,256]{1,0:T(8,128)S(1)}, u32[]{:S(2)}, u32[]{:S(2)}) collective-permute-start(f32[64,256]{1,0:T(8,128)S(1)} %get-tuple-element.28), channel_id=1, source_target_pairs={{0,6},{1,7},{2,4},{3,5},{4,2},{5,3},{6,0},{7,1},{8,14},{9,15},{10,... | collective-permute-start | bytes 196616 | tf_op jit(solution)/shard_map/ppermute | solution.py:25
  33.7 4.9 %collective-permute-start.13 = (f32[32,256]{1,0:T(8,128)S(1)}, f32[32,256]{1,0:T(8,128)S(1)}, u32[]{:S(2)}, u32[]{:S(2)}) collective-permute-start(f32[32,256]{1,0:T(8,128)S(1)} %get-tuple-element.30), channel_id=1, source_target_pairs={{0,8},{1,9},{2,10},{3,11},{4,12},{5,13},{6,14},{7,15},{8,0},{9,1},... | collective-permute-start | bytes 98312 | tf_op jit(solution)/shard_map/ppermute | solution.py:25

commit v4 on v3

--- a/solution.py
+++ b/solution.py
@@ -10,6 +10,8 @@
 NCH = 2
 CW = 256
 MIB = 2**20
+EARLY = ("own", "a", "d")
+PASSES = 3
 QUAD = ((0, 0), (1, 2), (2, 1), (3, 3))
 SMEM = pl.BlockSpec(memory_space=pltpu.SMEM)
 VMEM = pl.BlockSpec(memory_space=pltpu.VMEM)
@@ -52,33 +54,23 @@
         copy.wait()
 
 
-def after_kernel(block_ref, after_ref, out_ref):
-    out_ref[...] = block_ref[...]
-
-
-def join_kernel(low_ref, high_ref, after_ref, out_ref):
+def join_kernel(low_ref, high_ref, out_ref):
     rows = low_ref.shape[0]
     out_ref[:rows] = low_ref[...]
     out_ref[rows:] = high_ref[...]
 
 
-def product_kernel(n, places, coupling_ref, mine_z, other_z, other_own, *refs):
-    block_refs = refs[:-4]
-    mine_ref, other_ref, send_ref, keep_ref = refs[-4:]
-    rows = mine_z.shape[0]
+def accumulate(places, coupling_ref, z_refs, block_refs, total_refs):
+    rows = z_refs[0].shape[0]
     me = lax.axis_index("row")
     core = lax.rem(me, 2)
     children = (coupling_ref[me], coupling_ref[me ^ 1])
-    for total_ref in (mine_ref, other_ref):
-        total_ref[...] = jnp.zeros_like(total_ref)
     for held, block_ref in zip(places, block_refs):
         for number, (even, odd) in enumerate(held):
             tile = me ^ jnp.where(core == 0, even, odd)
             tile_child = coupling_ref[tile]
             columns = pl.ds(pl.multiple_of(lax.div(tile, 2) * rows, rows), rows)
-            for child, z_ref, total_ref in zip(
-                children, (mine_z, other_z), (mine_ref, other_ref)
-            ):
+            for child, z_ref, total_ref in zip(children, z_refs, total_refs):
 
                 @pl.when((tile_child == child) & (child < NCH))
                 def _():
@@ -88,20 +80,36 @@
                         preferred_element_type=jnp.float32,
                     )
 
+    return core, children
+
+
+def early_kernel(places, coupling_ref, mine_z, other_z, other_own, own_ref, *refs):
+    block_refs = refs[:-4]
+    mine_ref, other_ref, own_t, other_t = refs[-4:]
+    own_t[...] = own_ref[...].T
+    other_t[...] = other_own[...].T
+    for total_ref in (mine_ref, other_ref):
+        total_ref[...] = jnp.zeros_like(total_ref)
+    accumulate(places, coupling_ref, (mine_z, other_z), block_refs, (mine_ref, other_ref))
+
+
+def product_kernel(n, places, coupling_ref, mine_z, other_z, *refs):
+    mine_part, other_part, own_t, other_t = refs[:4]
+    mine_ref, other_ref, send_ref, keep_ref = refs[-4:]
+    mine_ref[...] = mine_part[...]
+    other_ref[...] = other_part[...]
+    core, children = accumulate(
+        places, coupling_ref, (mine_z, other_z), refs[4:-4], (mine_ref, other_ref)
+    )
     terms = []
-    for left_ref, total_ref in ((block_refs[0], mine_ref), (other_own, other_ref)):
-        total = total_ref[...]
-        high = total.astype(jnp.bfloat16)
-        low = (total - high.astype(jnp.float32)).astype(jnp.bfloat16)
-        left = left_ref[...]
-        terms.append(
-            sum(
-                lax.dot_general(
-                    left, part, (((0,), (0,)), ((), ())), preferred_element_type=jnp.float32
-                )
-                for part in (high, low)
-            )
-        )
+    for left_ref, total_ref in ((own_t, mine_ref), (other_t, other_ref)):
+        rest = total_ref[...]
+        term = jnp.zeros((CW, CW), jnp.float32)
+        for _ in range(PASSES):
+            part = rest.astype(jnp.bfloat16)
+            rest = rest - part.astype(jnp.float32)
+            term += jnp.dot(left_ref[...], part, preferred_element_type=jnp.float32)
+        terms.append(term)
     piece = NCH * CW // n
     zero = jnp.zeros((piece, CW), jnp.float32)
     for child in range(NCH):
@@ -155,17 +163,6 @@
     diag_ref[...] = inverse_ref[...] + (kept_ref[...] + got_ref[...])
 
 
-def after(block, other):
-    return pl.pallas_call(
-        after_kernel,
-        out_shape=pltpu.VMEM(block.shape, block.dtype),
-        in_specs=[VMEM, ANY],
-        out_specs=VMEM,
-        compiler_params=params(2),
-        name="after",
-    )(block, other)
-
-
 def gather(block, inverse_root, n):
     rows = block.shape[0]
     held = {"own": ([(0, 0)], block)}
@@ -188,17 +185,17 @@
         in_specs=[ANY, ANY],
         out_specs=[VMEM] * 2,
         scratch_shapes=[pltpu.SemaphoreType.DMA((n // 2, 2))],
-        compiler_params=params(62 - inverse_root.size * 2 // MIB),
+        compiler_params=params(60 - inverse_root.size * 2 // MIB),
         name="load",
     )(inverse_root, other_z)
     pair = pl.pallas_call(
         join_kernel,
         out_shape=pltpu.VMEM((2 * rows, CW), block.dtype),
-        in_specs=[VMEM, VMEM, ANY],
+        in_specs=[VMEM, VMEM],
         out_specs=VMEM,
         compiler_params=params(2),
         name="join",
-    )(block, held["a"][1], mine_z)
+    )(block, held["a"][1])
     held["pair"] = (held["own"][0] + held["a"][0], pair)
     fetch("bc", "pair", (4, 2))
     del held["pair"]
@@ -208,7 +205,7 @@
     for bit in range(4, n.bit_length() - 1):
         for name in list(held):
             fetch(f"{name}_{bit}", name, (1 << bit, 1 << bit))
-    return mine_z, other_z, other_own, list(held.values())
+    return mine_z, other_z, other_own, held
 
 
 def per_device(n, inverse_root, lower_panel, coupling, child_inverse):
@@ -222,19 +219,32 @@
         name="compact",
     )(coupling, lower_panel)
     mine_z, other_z, other_own, held = gather(block, inverse_root, n)
+    late = [name for name in held if name not in EARLY]
+    square = jax.ShapeDtypeStruct((rows, CW), jnp.float32)
+    turned = jax.ShapeDtypeStruct((CW, rows), block.dtype)
+    partial = pl.pallas_call(
+        functools.partial(early_kernel, [held[name][0] for name in EARLY]),
+        out_shape=[square, square, turned, turned],
+        in_specs=[SMEM] + [VMEM] * (len(EARLY) + 4),
+        out_specs=[VMEM] * 4,
+        compiler_params=params(24 if n > 16 else 8),
+        name="early",
+    )(coupling, mine_z, other_z, other_own, block, *[held[name][1] for name in EARLY])
     mine, other, send, keep = pl.pallas_call(
-        functools.partial(product_kernel, n, [places for places, _ in held]),
-        out_shape=[
-            jax.ShapeDtypeStruct((rows, CW), jnp.float32),
-            jax.ShapeDtypeStruct((rows, CW), jnp.float32),
-            jax.ShapeDtypeStruct((NCH * CW // 2, CW), jnp.float32),
-            jax.ShapeDtypeStruct((NCH * CW // 2, CW), jnp.float32),
-        ],
-        in_specs=[SMEM] + [VMEM] * (len(held) + 3),
+        functools.partial(product_kernel, n, [held[name][0] for name in late]),
+        out_shape=[square, square]
+        + [jax.ShapeDtypeStruct((NCH * CW // 2, CW), jnp.float32)] * 2,
+        in_specs=[SMEM] + [VMEM] * (len(late) + 6),
         out_specs=[VMEM] * 4,
         compiler_params=params(24 if n > 16 else 8),
         name="product",
-    )(coupling, mine_z, other_z, other_own, *[block for _, block in held])
+    )(
+        coupling,
+        mine_z,
+        other_z,
+        *partial,
+        *[held[name][1] for name in late],
+    )
     got = exchange(send, n, (1, 1))
     piece = NCH * CW // n
     width = NCH * CW // 2 // len(QUAD)
@@ -246,14 +256,6 @@
         compiler_params=params(2),
         name="quad",
     )(keep, got))
-    offdiag, token = pl.pallas_call(
-        offdiag_kernel,
-        out_shape=[jax.ShapeDtypeStruct((rows, NCH * CW), jnp.float32), TOKEN],
-        in_specs=[SMEM, VMEM, VMEM],
-        out_specs=[VMEM] * 2,
-        compiler_params=params(4),
-        name="offdiag",
-    )(coupling, mine, exchange(after(other, parts[0]), n, (1, 1)))
     for number in range(1, len(QUAD)):
         parts[number] = exchange(parts[number], n, tuple(2 * m for m in QUAD[number]))
     for bit in range(2, (n // 2).bit_length() - 1):
@@ -268,6 +270,14 @@
         )(*parts)
         got = exchange(send, n, (2 << bit, 2 << bit))
         parts = [keep, got]
+    offdiag, token = pl.pallas_call(
+        offdiag_kernel,
+        out_shape=[jax.ShapeDtypeStruct((rows, NCH * CW), jnp.float32), TOKEN],
+        in_specs=[SMEM, VMEM, VMEM],
+        out_specs=[VMEM] * 2,
+        compiler_params=params(4),
+        name="offdiag",
+    )(coupling, mine, exchange(other, n, (1, 1)))
     child_diag = pl.pallas_call(
         last_kernel,
         out_shape=jax.ShapeDtypeStruct((piece, CW), jnp.float32),

time: 39.1 us -> 38.5 us (0.985)
  waiting for transfers between devices: 15.2 us -> 11.6 us
  Pallas kernels: 6.62 us -> 8.05 us
  starting transfers between devices: 16.6 us -> 17.8 us
    ppermute x14, waiting for transfers between devices: 15.2 us -> 11.6 us  [exchange(): return lax.ppermute(block, 'row', [(i, i ^ masks[i % 2]) for i in range(n)])]
    pallas_call x2, Pallas kernels: 1.79 us -> 3.23 us  [the longest x1 1.79 us: per_device(): pl.pallas_call(functools.partial(early_kernel, [held[name][0] for name in...]
    ppermute x14, starting transfers between devices: 16.6 us -> 17.8 us  [exchange(): return lax.ppermute(block, 'row', [(i, i ^ masks[i % 2]) for i in range(n)])]
  transfers between devices with their start and end apart: 14 -> 14, of which waited for: 8 -> 9; matrix products, arithmetic and copies ran while one was open for 0% -> 0% of each run, Pallas kernels for 8% -> 13%
where the time goes in v4:
time: 38.5 us; the launch traced here: 38.2 us
  starting transfers between devices  17.8 us (46%)
  waiting for transfers between devices  11.6 us (30%)
  Pallas kernels  8.05 us (21%)
  between operations  0.72 us (2%)
    ppermute x14, starting transfers between devices, exchange(): return lax.ppermute(block, 'row', [(i, i ^ masks[i % 2]) for i in range(n)])  17.8 us
    ppermute x14, waiting for transfers between devices, exchange(): return lax.ppermute(block, 'row', [(i, i ^ masks[i % 2]) for i in range(n)])  11.6 us
    pallas_call x1, Pallas kernels, per_device(): pl.pallas_call(functools.partial(early_kernel, [held[name][0] for name in...  1.79 us
    pallas_call x1, Pallas kernels, gather(): pl.pallas_call(load_kernel, out_shape=[half, half], in_specs=[ANY, ANY],...  1.76 us
    pallas_call x1, Pallas kernels, per_device(): pl.pallas_call(functools.partial(product_kernel, n, [held[name][0] for na...  1.44 us
    pallas_call x1, Pallas kernels, per_device(): pl.pallas_call(offdiag_kernel, out_shape=[jax.ShapeDtypeStruct((rows, NCH...  1.39 us
    pallas_call x1, Pallas kernels, per_device(): pl.pallas_call(compact_kernel, out_shape=pltpu.VMEM((rows, CW), lower_pan...  0.98 us
  transfers between devices with their start and end apart: 14, of which 9 were waited for; matrix products, arithmetic and copies ran while one was open for 0% of the time, Pallas kernels for 13%

profile of v4, /device:TPU:0, one launch (start us, length us, event | category | flops | bytes accessed | tf_op | source)
XLA Modules:
  0.0 38.2 jit_solution(12490103290872556347)
XLA Ops:
  0.6 1.0 %compact.1.own_ref.refs_0_.low_ref = bf16[256,256]{1,0:T(8,128)(2,1)S(1)} custom-call(s32[16]{0:T(128)} %coupling_ref.7, bf16[256,512]{1,0:T(8,128)(2,1)} %panel_ref.1), custom_call_target="tpu_custom_call" | custom-call | tf_op jit(solution)/shard_map/compact/pallas_call | solution.py:213
  1.6 0.5 %collective-permute-start = (bf16[256,4096]{1,0:T(8,128)(2,1)}, bf16[256,4096]{1,0:T(8,128)(2,1)S(1)}, u32[]{:S(2)}, u32[]{:S(2)}) collective-permute-start(bf16[256,4096]{1,0:T(8,128)(2,1)} %mine_hbm.1), channel_id=1, source_target_pairs={{0,1},{1,0},{2,3},{3,2},{4,5},{5,4},{6,7},{7,6},{8,9},{9,8},{10,11... | collective-permute-start | bytes 6291464 | tf_op jit(solution)/shard_map/ppermute | solution.py:27
  2.1 2.6 %collective-permute-start.2 = (bf16[256,256]{1,0:T(8,128)(2,1)S(1)}, bf16[256,256]{1,0:T(8,128)(2,1)S(1)}, u32[]{:S(2)}, u32[]{:S(2)}) collective-permute-start(bf16[256,256]{1,0:T(8,128)(2,1)S(1)} %compact.1.own_ref.refs_0_.low_ref), channel_id=1, source_target_pairs={{0,2},{1,5},{2,0},{3,7},{4,6},{5,1},{6,4},{7,3},{8,10},{9,13},{10,... | collective-permute-start | bytes 393224 | tf_op jit(solution)/shard_map/ppermute | solution.py:27
  4.7 2.6 %collective-permute-start.3 = (bf16[256,256]{1,0:T(8,128)(2,1)S(1)}, bf16[256,256]{1,0:T(8,128)(2,1)S(1)}, u32[]{:S(2)}, u32[]{:S(2)}) collective-permute-start(bf16[256,256]{1,0:T(8,128)(2,1)S(1)} %compact.1.own_ref.refs_0_.low_ref), channel_id=1, source_target_pairs={{0,8},{1,9},{2,10},{3,11},{4,12},{5,13},{6,14},{7,15},{8,0},{9,1},... | collective-permute-start | bytes 393224 | tf_op jit(solution)/shard_map/ppermute | solution.py:27
  7.3 0.4 collective-permute-done.2.refs_1_.high_ref
  7.7 0.0 copy-start.1
  7.7 2.1 %collective-permute-start.4 = (bf16[512,256]{1,0:T(8,128)(2,1)S(1)}, bf16[512,256]{1,0:T(8,128)(2,1)S(1)}, u32[]{:S(2)}, u32[]{:S(2)}) collective-permute-start(bf16[512,256]{1,0:T(8,128)(2,1)S(1)} %join.1), channel_id=1, source_target_pairs={{0,4},{1,3},{2,6},{3,1},{4,0},{5,7},{6,2},{7,5},{8,12},{9,11},{10,... | collective-permute-start | bytes 786440 | tf_op jit(solution)/shard_map/ppermute | solution.py:27
  9.9 0.0 collective-permute-start.1
  9.9 4.3 %collective-permute-done.3.refs_2_ = bf16[256,256]{1,0:T(8,128)(2,1)S(1)} collective-permute-done((bf16[256,256]{1,0:T(8,128)(2,1)S(1)}, bf16[256,256]{1,0:T(8,128)(2,1)S(1)}, u32[]{:S(2)}, u32[]{:S(2)}) %collective-permute-start.3) | collective-permute-done | bytes 131104 | tf_op jit(solution)/shard_map/ppermute | solution.py:27
  14.2 0.5 %collective-permute-start.5 = (bf16[256,256]{1,0:T(8,128)(2,1)S(1)}, bf16[256,256]{1,0:T(8,128)(2,1)S(1)}, u32[]{:S(2)}, u32[]{:S(2)}) collective-permute-start(bf16[256,256]{1,0:T(8,128)(2,1)S(1)} %collective-permute-done.3.refs_2_), channel_id=1, source_target_pairs={{0,6},{1,7},{2,4},{3,5},{4,2},{5,3},{6,0},{7,1},{8,14},{9,15},{10,... | collective-permute-start | bytes 393224 | tf_op jit(solution)/shard_map/ppermute | solution.py:27
  14.7 0.6 %collective-permute-start.6 = (bf16[256,256]{1,0:T(8,128)(2,1)S(1)}, bf16[256,256]{1,0:T(8,128)(2,1)S(1)}, u32[]{:S(2)}, u32[]{:S(2)}) collective-permute-start(bf16[256,256]{1,0:T(8,128)(2,1)S(1)} %collective-permute-done.3.refs_2_), channel_id=1, source_target_pairs={{0,2},{1,5},{2,0},{3,7},{4,6},{5,1},{6,4},{7,3},{8,10},{9,13},{10,... | collective-permute-start | bytes 393224 | tf_op jit(solution)/shard_map/ppermute | solution.py:27
  15.2 0.0 collective-permute-done.other_hbm
  15.2 0.0 copy-start.2
  15.2 2.4 %collective-permute-start.7 = (bf16[256,256]{1,0:T(8,128)(2,1)S(1)}, bf16[256,256]{1,0:T(8,128)(2,1)S(1)}, u32[]{:S(2)}, u32[]{:S(2)}) collective-permute-start(bf16[256,256]{1,0:T(8,128)(2,1)S(1)} %collective-permute-done.3.refs_2_), channel_id=1, source_target_pairs={{0,4},{1,3},{2,6},{3,1},{4,0},{5,7},{6,2},{7,5},{8,12},{9,11},{10,... | collective-permute-start | bytes 393224 | tf_op jit(solution)/shard_map/ppermute | solution.py:27
  17.7 0.0 copy-done.2
  17.7 1.8 %load.1 = (bf16[256,2048]{1,0:T(8,128)(2,1)S(1)}, bf16[256,2048]{1,0:T(8,128)(2,1)S(1)}) custom-call(bf16[256,4096]{1,0:T(8,128)(2,1)} %mine_hbm.1, bf16[256,4096]{1,0:T(8,128)(2,1)} %copy-done.2), custom_call_target="tpu_custom_call" | custom-call | tf_op jit(solution)/shard_map/load/pallas_call | solution.py:182
  19.4 0.0 collective-permute-done.1.other_own
  19.4 0.0 copy-done.1
  19.4 1.8 %early.1 = (f32[256,256]{1,0:T(8,128)S(1)}, f32[256,256]{1,0:T(8,128)S(1)}, bf16[256,256]{1,0:T(8,128)(2,1)S(1)}, bf16[256,256]{1,0:T(8,128)(2,1)S(1)}) custom-call(s32[16]{0:T(128)S(1)} %copy-done.1, bf16[256,2048]{1,0:T(8,128)(2,1)S(1)} %get-tuple-element.22.mine_z, bf16[256,2048]{1,0:T(8,128)(2,1)S(1)} %get-tuple-element.23.other_z, ...), custom_call_target="tpu_custom_call" | custom-call | tf_op jit(solution)/shard_map/early/pallas_call | solution.py:225
  21.2 0.0 collective-permute-done.5.refs_5_
  21.3 1.2 %collective-permute-done.6.refs_6_ = bf16[256,256]{1,0:T(8,128)(2,1)S(1)} collective-permute-done((bf16[256,256]{1,0:T(8,128)(2,1)S(1)}, bf16[256,256]{1,0:T(8,128)(2,1)S(1)}, u32[]{:S(2)}, u32[]{:S(2)}) %collective-permute-start.6) | collective-permute-done | bytes 131104 | tf_op jit(solution)/shard_map/ppermute | solution.py:27
  22.4 0.2 collective-permute-done.7.refs_7_
  22.6 0.0 collective-permute-done.4.refs_4_
  22.6 0.0 copy-start
  22.6 1.4 %product.1 = (f32[256,256]{1,0:T(8,128)S(1)}, f32[256,256]{1,0:T(8,128)S(1)}, f32[256,256]{1,0:T(8,128)S(1)}, f32[256,256]{1,0:T(8,128)S(1)}) custom-call(s32[16]{0:T(128)S(1)} %copy-done.1, bf16[256,2048]{1,0:T(8,128)(2,1)S(1)} %get-tuple-element.22.mine_z, bf16[256,2048]{1,0:T(8,128)(2,1)S(1)} %get-tuple-element.23.other_z, ...), custom_call_target="tpu_custom_call" | custom-call | tf_op jit(solution)/shard_map/product/pallas_call | solution.py:233
  24.1 0.5 %collective-permute-start.9 = (f32[256,256]{1,0:T(8,128)S(1)}, f32[256,256]{1,0:T(8,128)S(1)}, u32[]{:S(2)}, u32[]{:S(2)}) collective-permute-start(f32[256,256]{1,0:T(8,128)S(1)} %get-tuple-element.32), channel_id=1, source_target_pairs={{0,1},{1,0},{2,3},{3,2},{4,5},{5,4},{6,7},{7,6},{8,9},{9,8},{10,11... | collective-permute-start | bytes 786440 | tf_op jit(solution)/shard_map/ppermute | solution.py:27
  24.5 0.1 collective-permute-start.8
  24.6 1.1 %collective-permute-done.9.got_ref = f32[256,256]{1,0:T(8,128)S(1)} collective-permute-done((f32[256,256]{1,0:T(8,128)S(1)}, f32[256,256]{1,0:T(8,128)S(1)}, u32[]{:S(2)}, u32[]{:S(2)}) %collective-permute-start.9) | collective-permute-done | bytes 262176 | tf_op jit(solution)/shard_map/ppermute | solution.py:27
  25.7 1.4 %collective-permute-start.10 = (f32[64,256]{1,0:T(8,128)S(1)}, f32[64,256]{1,0:T(8,128)S(1)}, u32[]{:S(2)}, u32[]{:S(2)}) collective-permute-start(f32[64,256]{1,0:T(8,128)S(1)} %get-tuple-element.34), channel_id=1, source_target_pairs={{0,2},{1,5},{2,0},{3,7},{4,6},{5,1},{6,4},{7,3},{8,10},{9,13},{10,... | collective-permute-start | bytes 196616 | tf_op jit(solution)/shard_map/ppermute | solution.py:27
  27.1 0.0 collective-permute-start.11
  27.2 2.1 %collective-permute-start.12 = (f32[64,256]{1,0:T(8,128)S(1)}, f32[64,256]{1,0:T(8,128)S(1)}, u32[]{:S(2)}, u32[]{:S(2)}) collective-permute-start(f32[64,256]{1,0:T(8,128)S(1)} %get-tuple-element.36), channel_id=1, source_target_pairs={{0,6},{1,7},{2,4},{3,5},{4,2},{5,3},{6,0},{7,1},{8,14},{9,15},{10,... | collective-permute-start | bytes 196616 | tf_op jit(solution)/shard_map/ppermute | solution.py:27
  29.3 1.0 %collective-permute-done.10.refs_1_ = f32[64,256]{1,0:T(8,128)S(1)} collective-permute-done((f32[64,256]{1,0:T(8,128)S(1)}, f32[64,256]{1,0:T(8,128)S(1)}, u32[]{:S(2)}, u32[]{:S(2)}) %collective-permute-start.10) | collective-permute-done | bytes 65568 | tf_op jit(solution)/shard_map/ppermute | solution.py:27
  30.3 1.2 %collective-permute-done.11.refs_2_ = f32[64,256]{1,0:T(8,128)S(1)} collective-permute-done((f32[64,256]{1,0:T(8,128)S(1)}, f32[64,256]{1,0:T(8,128)S(1)}, u32[]{:S(2)}, u32[]{:S(2)}) %collective-permute-start.11) | collective-permute-done | bytes 65568 | tf_op jit(solution)/shard_map/ppermute | solution.py:27
  31.4 1.2 %collective-permute-done.12.refs_3_ = f32[64,256]{1,0:T(8,128)S(1)} collective-permute-done((f32[64,256]{1,0:T(8,128)S(1)}, f32[64,256]{1,0:T(8,128)S(1)}, u32[]{:S(2)}, u32[]{:S(2)}) %collective-permute-start.12) | collective-permute-done | bytes 65568 | tf_op jit(solution)/shard_map/ppermute | solution.py:27
  32.7 2.4 %collective-permute-start.13 = (f32[32,256]{1,0:T(8,128)S(1)}, f32[32,256]{1,0:T(8,128)S(1)}, u32[]{:S(2)}, u32[]{:S(2)}) collective-permute-start(f32[32,256]{1,0:T(8,128)S(1)} %get-tuple-element.38), channel_id=1, source_target_pairs={{0,8},{1,9},{2,10},{3,11},{4,12},{5,13},{6,14},{7,15},{8,0},{9,1},... | collective-permute-start | bytes 98312 | tf_op jit(solution)/shard_map/ppermute | solution.py:27
  35.1 0.0 collective-permute-done.8.other_ref
  35.1 1.4 %offdiag.1 = (f32[256,512]{1,0:T(8,128)}, f32[8,128]{1,0:T(8,128)S(1)}) custom-call(s32[16]{0:T(128)S(1)} %copy-done.1, f32[256,256]{1,0:T(8,128)S(1)} %get-tuple-element.28.mine_ref, f32[256,256]{1,0:T(8,128)S(1)} %collective-permute-done.8.other_ref), custom_call_target="tpu_custom_call" | custom-call | tf_op jit(solution)/shard_map/offdiag/pallas_call | solution.py:273
  36.5 1.1 %collective-permute-done.13.got_ref = f32[32,256]{1,0:T(8,128)S(1)} collective-permute-done((f32[32,256]{1,0:T(8,128)S(1)}, f32[32,256]{1,0:T(8,128)S(1)}, u32[]{:S(2)}, u32[]{:S(2)}) %collective-permute-start.13) | collective-permute-done | bytes 32800 | tf_op jit(solution)/shard_map/ppermute | solution.py:27
  37.6 0.0 copy-done
  37.6 0.6 %last.1 = f32[32,256]{1,0:T(8,128)} custom-call(f32[32,256]{1,0:T(8,128)S(1)} %copy-done, f32[32,256]{1,0:T(8,128)S(1)} %get-tuple-element.37.kept_ref, f32[32,256]{1,0:T(8,128)S(1)} %collective-permute-done.13.got_ref, f32[8,128]{1,0:T(8,128)S(1)} %get-tuple-element.39.after_ref), custom_call_target="tpu_custom_call" | custom-call | tf_op jit(solution)/shard_map/last/pallas_call | solution.py:281
  (3 shorter events, 0.1 us)
Async XLA Ops:
  1.6 13.6 %collective-permute-start = (bf16[256,4096]{1,0:T(8,128)(2,1)}, bf16[256,4096]{1,0:T(8,128)(2,1)S(1)}, u32[]{:S(2)}, u32[]{:S(2)}) collective-permute-start(bf16[256,4096]{1,0:T(8,128)(2,1)} %mine_hbm.1), channel_id=1, source_target_pairs={{0,1},{1,0},{2,3},{3,2},{4,5},{5,4},{6,7},{7,6},{8,9},{9,8},{10,11... | collective-permute-start | bytes 6291464 | tf_op jit(solution)/shard_map/ppermute | solution.py:27
  2.1 5.5 %collective-permute-start.2 = (bf16[256,256]{1,0:T(8,128)(2,1)S(1)}, bf16[256,256]{1,0:T(8,128)(2,1)S(1)}, u32[]{:S(2)}, u32[]{:S(2)}) collective-permute-start(bf16[256,256]{1,0:T(8,128)(2,1)S(1)} %compact.1.own_ref.refs_0_.low_ref), channel_id=1, source_target_pairs={{0,2},{1,5},{2,0},{3,7},{4,6},{5,1},{6,4},{7,3},{8,10},{9,13},{10,... | collective-permute-start | bytes 393224 | tf_op jit(solution)/shard_map/ppermute | solution.py:27
  4.7 9.4 %collective-permute-start.3 = (bf16[256,256]{1,0:T(8,128)(2,1)S(1)}, bf16[256,256]{1,0:T(8,128)(2,1)S(1)}, u32[]{:S(2)}, u32[]{:S(2)}) collective-permute-start(bf16[256,256]{1,0:T(8,128)(2,1)S(1)} %compact.1.own_ref.refs_0_.low_ref), channel_id=1, source_target_pairs={{0,8},{1,9},{2,10},{3,11},{4,12},{5,13},{6,14},{7,15},{8,0},{9,1},... | collective-permute-start | bytes 393224 | tf_op jit(solution)/shard_map/ppermute | solution.py:27
  7.7 11.7 %copy-start.1 = (s32[16]{0:T(128)S(1)}, s32[16]{0:T(128)}, u32[]{:S(2)}) copy-start(s32[16]{0:T(128)} %coupling_ref.7) | copy-start | bytes 196
  7.7 14.9 %collective-permute-start.4 = (bf16[512,256]{1,0:T(8,128)(2,1)S(1)}, bf16[512,256]{1,0:T(8,128)(2,1)S(1)}, u32[]{:S(2)}, u32[]{:S(2)}) collective-permute-start(bf16[512,256]{1,0:T(8,128)(2,1)S(1)} %join.1), channel_id=1, source_target_pairs={{0,4},{1,3},{2,6},{3,1},{4,0},{5,7},{6,2},{7,5},{8,12},{9,11},{10,... | collective-permute-start | bytes 786440 | tf_op jit(solution)/shard_map/ppermute | solution.py:27
  9.9 9.6 %collective-permute-start.1 = (bf16[256,256]{1,0:T(8,128)(2,1)S(1)}, bf16[256,256]{1,0:T(8,128)(2,1)S(1)}, u32[]{:S(2)}, u32[]{:S(2)}) collective-permute-start(bf16[256,256]{1,0:T(8,128)(2,1)S(1)} %compact.1.own_ref.refs_0_.low_ref), channel_id=1, source_target_pairs={{0,1},{1,0},{2,3},{3,2},{4,5},{5,4},{6,7},{7,6},{8,9},{9,8},{10,11... | collective-permute-start | bytes 393224 | tf_op jit(solution)/shard_map/ppermute | solution.py:27
  14.2 7.1 %collective-permute-start.5 = (bf16[256,256]{1,0:T(8,128)(2,1)S(1)}, bf16[256,256]{1,0:T(8,128)(2,1)S(1)}, u32[]{:S(2)}, u32[]{:S(2)}) collective-permute-start(bf16[256,256]{1,0:T(8,128)(2,1)S(1)} %collective-permute-done.3.refs_2_), channel_id=1, source_target_pairs={{0,6},{1,7},{2,4},{3,5},{4,2},{5,3},{6,0},{7,1},{8,14},{9,15},{10,... | collective-permute-start | bytes 393224 | tf_op jit(solution)/shard_map/ppermute | solution.py:27
  14.7 7.8 %collective-permute-start.6 = (bf16[256,256]{1,0:T(8,128)(2,1)S(1)}, bf16[256,256]{1,0:T(8,128)(2,1)S(1)}, u32[]{:S(2)}, u32[]{:S(2)}) collective-permute-start(bf16[256,256]{1,0:T(8,128)(2,1)S(1)} %collective-permute-done.3.refs_2_), channel_id=1, source_target_pairs={{0,2},{1,5},{2,0},{3,7},{4,6},{5,1},{6,4},{7,3},{8,10},{9,13},{10,... | collective-permute-start | bytes 393224 | tf_op jit(solution)/shard_map/ppermute | solution.py:27
  15.2 2.4 %copy-start.2 = (bf16[256,4096]{1,0:T(8,128)(2,1)}, bf16[256,4096]{1,0:T(8,128)(2,1)S(1)}, u32[]{:S(2)}) copy-start(bf16[256,4096]{1,0:T(8,128)(2,1)S(1)} %collective-permute-done.other_hbm) | copy-start | bytes 6291460
  15.2 7.4 %collective-permute-start.7 = (bf16[256,256]{1,0:T(8,128)(2,1)S(1)}, bf16[256,256]{1,0:T(8,128)(2,1)S(1)}, u32[]{:S(2)}, u32[]{:S(2)}) collective-permute-start(bf16[256,256]{1,0:T(8,128)(2,1)S(1)} %collective-permute-done.3.refs_2_), channel_id=1, source_target_pairs={{0,4},{1,3},{2,6},{3,1},{4,0},{5,7},{6,2},{7,5},{8,12},{9,11},{10,... | collective-permute-start | bytes 393224 | tf_op jit(solution)/shard_map/ppermute | solution.py:27
  22.6 15.0 %copy-start = (f32[32,256]{1,0:T(8,128)S(1)}, f32[32,256]{1,0:T(8,128)}, u32[]{:S(2)}) copy-start(f32[32,256]{1,0:T(8,128)} %inverse_ref.1) | copy-start | bytes 98308
  24.1 1.6 %collective-permute-start.9 = (f32[256,256]{1,0:T(8,128)S(1)}, f32[256,256]{1,0:T(8,128)S(1)}, u32[]{:S(2)}, u32[]{:S(2)}) collective-permute-start(f32[256,256]{1,0:T(8,128)S(1)} %get-tuple-element.32), channel_id=1, source_target_pairs={{0,1},{1,0},{2,3},{3,2},{4,5},{5,4},{6,7},{7,6},{8,9},{9,8},{10,11... | collective-permute-start | bytes 786440 | tf_op jit(solution)/shard_map/ppermute | solution.py:27
  24.5 10.5 %collective-permute-start.8 = (f32[256,256]{1,0:T(8,128)S(1)}, f32[256,256]{1,0:T(8,128)S(1)}, u32[]{:S(2)}, u32[]{:S(2)}) collective-permute-start(f32[256,256]{1,0:T(8,128)S(1)} %get-tuple-element.29), channel_id=1, source_target_pairs={{0,1},{1,0},{2,3},{3,2},{4,5},{5,4},{6,7},{7,6},{8,9},{9,8},{10,11... | collective-permute-start | bytes 786440 | tf_op jit(solution)/shard_map/ppermute | solution.py:27
  25.7 4.5 %collective-permute-start.10 = (f32[64,256]{1,0:T(8,128)S(1)}, f32[64,256]{1,0:T(8,128)S(1)}, u32[]{:S(2)}, u32[]{:S(2)}) collective-permute-start(f32[64,256]{1,0:T(8,128)S(1)} %get-tuple-element.34), channel_id=1, source_target_pairs={{0,2},{1,5},{2,0},{3,7},{4,6},{5,1},{6,4},{7,3},{8,10},{9,13},{10,... | collective-permute-start | bytes 196616 | tf_op jit(solution)/shard_map/ppermute | solution.py:27
  27.1 4.3 %collective-permute-start.11 = (f32[64,256]{1,0:T(8,128)S(1)}, f32[64,256]{1,0:T(8,128)S(1)}, u32[]{:S(2)}, u32[]{:S(2)}) collective-permute-start(f32[64,256]{1,0:T(8,128)S(1)} %get-tuple-element.35), channel_id=1, source_target_pairs={{0,4},{1,3},{2,6},{3,1},{4,0},{5,7},{6,2},{7,5},{8,12},{9,11},{10,... | collective-permute-start | bytes 196616 | tf_op jit(solution)/shard_map/ppermute | solution.py:27
  27.2 5.5 %collective-permute-start.12 = (f32[64,256]{1,0:T(8,128)S(1)}, f32[64,256]{1,0:T(8,128)S(1)}, u32[]{:S(2)}, u32[]{:S(2)}) collective-permute-start(f32[64,256]{1,0:T(8,128)S(1)} %get-tuple-element.36), channel_id=1, source_target_pairs={{0,6},{1,7},{2,4},{3,5},{4,2},{5,3},{6,0},{7,1},{8,14},{9,15},{10,... | collective-permute-start | bytes 196616 | tf_op jit(solution)/shard_map/ppermute | solution.py:27
  32.7 4.9 %collective-permute-start.13 = (f32[32,256]{1,0:T(8,128)S(1)}, f32[32,256]{1,0:T(8,128)S(1)}, u32[]{:S(2)}, u32[]{:S(2)}) collective-permute-start(f32[32,256]{1,0:T(8,128)S(1)} %get-tuple-element.38), channel_id=1, source_target_pairs={{0,8},{1,9},{2,10},{3,11},{4,12},{5,13},{6,14},{7,15},{8,0},{9,1},... | collective-permute-start | bytes 98312 | tf_op jit(solution)/shard_map/ppermute | solution.py:27

commit v5 on v4

--- a/solution.py
+++ b/solution.py
@@ -12,7 +12,8 @@
 MIB = 2**20
 EARLY = ("own", "a", "d")
 PASSES = 3
-QUAD = ((0, 0), (1, 2), (2, 1), (3, 3))
+QUAD = ((0, 0), (3, 3), (1, 2), (2, 1))
+BITS = 24
 SMEM = pl.BlockSpec(memory_space=pltpu.SMEM)
 VMEM = pl.BlockSpec(memory_space=pltpu.VMEM)
 ANY = pl.BlockSpec(memory_space=pl.ANY)
@@ -60,47 +61,71 @@
     out_ref[rows:] = high_ref[...]
 
 
-def accumulate(places, coupling_ref, z_refs, block_refs, total_refs):
-    rows = z_refs[0].shape[0]
+def walk(places, block_refs):
     me = lax.axis_index("row")
     core = lax.rem(me, 2)
-    children = (coupling_ref[me], coupling_ref[me ^ 1])
     for held, block_ref in zip(places, block_refs):
         for number, (even, odd) in enumerate(held):
-            tile = me ^ jnp.where(core == 0, even, odd)
-            tile_child = coupling_ref[tile]
-            columns = pl.ds(pl.multiple_of(lax.div(tile, 2) * rows, rows), rows)
-            for child, z_ref, total_ref in zip(children, z_refs, total_refs):
-
-                @pl.when((tile_child == child) & (child < NCH))
-                def _():
-                    total_ref[...] += jnp.dot(
-                        z_ref[:, columns],
-                        block_ref[number * rows:(number + 1) * rows],
-                        preferred_element_type=jnp.float32,
-                    )
-
-    return core, children
-
-
-def early_kernel(places, coupling_ref, mine_z, other_z, other_own, own_ref, *refs):
-    block_refs = refs[:-4]
-    mine_ref, other_ref, own_t, other_t = refs[-4:]
+            yield me ^ jnp.where(core == 0, even, odd), number, block_ref
+
+
+def accumulate(places, wanted, z_refs, block_refs, total_refs):
+    rows = z_refs[0].shape[0]
+    for at, (tile, number, block_ref) in enumerate(walk(places, block_refs)):
+        columns = pl.ds(pl.multiple_of(lax.div(tile, 2) * rows, rows), rows)
+        for side, (z_ref, total_ref) in enumerate(zip(z_refs, total_refs)):
+
+            @pl.when(wanted(at, side, tile))
+            def _():
+                total_ref[...] += jnp.dot(
+                    z_ref[:, columns],
+                    block_ref[number * rows:(number + 1) * rows],
+                    preferred_element_type=jnp.float32,
+                )
+
+
+def early_kernel(
+    places, late_places, coupling_ref, mine_z, other_z, other_own, own_ref, *refs
+):
+    block_refs = refs[:-5]
+    mine_ref, other_ref, own_t, other_t, flag_ref = refs[-5:]
+    me = lax.axis_index("row")
+    children = (coupling_ref[me], coupling_ref[me ^ 1])
+
+    def wanted(_, side, tile):
+        return (coupling_ref[tile] == children[side]) & (children[side] < NCH)
+
+    flags = [children[side] == child for child in range(NCH) for side in range(2)]
+    for tile, _, _ in walk(late_places, late_places):
+        flags += [wanted(None, side, tile) for side in range(2)]
+    for word in range(flag_ref.shape[0]):
+        value = jnp.int32(0)
+        for bit, flag in enumerate(flags[word * BITS:(word + 1) * BITS]):
+            value = value + jnp.where(flag, 1 << bit, 0)
+        flag_ref[word:word + 1] = jnp.full((1, 128), value, jnp.int32)
     own_t[...] = own_ref[...].T
     other_t[...] = other_own[...].T
     for total_ref in (mine_ref, other_ref):
         total_ref[...] = jnp.zeros_like(total_ref)
-    accumulate(places, coupling_ref, (mine_z, other_z), block_refs, (mine_ref, other_ref))
-
-
-def product_kernel(n, places, coupling_ref, mine_z, other_z, *refs):
-    mine_part, other_part, own_t, other_t = refs[:4]
+    accumulate(places, wanted, (mine_z, other_z), block_refs, (mine_ref, other_ref))
+
+
+def product_kernel(n, places, mine_z, other_z, *refs):
+    mine_part, other_part, own_t, other_t, flag_ref = refs[:5]
     mine_ref, other_ref, send_ref, keep_ref = refs[-4:]
+    count = 2 * (NCH + sum(len(held) for held in places))
+    words = [jnp.max(flag_ref[word:word + 1]) for word in range(-(-count // BITS))]
+    flags = [lax.rem(words[at // BITS] >> (at % BITS), 2) == 1 for at in range(count)]
     mine_ref[...] = mine_part[...]
     other_ref[...] = other_part[...]
-    core, children = accumulate(
-        places, coupling_ref, (mine_z, other_z), refs[4:-4], (mine_ref, other_ref)
+    accumulate(
+        places,
+        lambda at, side, _: flags[2 * (NCH + at) + side],
+        (mine_z, other_z),
+        refs[5:-4],
+        (mine_ref, other_ref),
     )
+    core = lax.rem(lax.axis_index("row"), 2)
     terms = []
     for left_ref, total_ref in ((own_t, mine_ref), (other_t, other_ref)):
         rest = total_ref[...]
@@ -116,8 +141,8 @@
         for q in range(CW // piece // 2):
             low, high = [
                 sum(
-                    jnp.where(mine == child, term[at:at + piece], zero)
-                    for mine, term in zip(children, terms)
+                    jnp.where(flags[2 * child + side], term[at:at + piece], zero)
+                    for side, term in enumerate(terms)
                 )
                 for at in (2 * q * piece, (2 * q + 1) * piece)
             ]
@@ -222,29 +247,33 @@
     late = [name for name in held if name not in EARLY]
     square = jax.ShapeDtypeStruct((rows, CW), jnp.float32)
     turned = jax.ShapeDtypeStruct((CW, rows), block.dtype)
+    late_places = [held[name][0] for name in late]
+    count = 2 * (NCH + sum(len(tiles) for tiles in late_places))
     partial = pl.pallas_call(
-        functools.partial(early_kernel, [held[name][0] for name in EARLY]),
-        out_shape=[square, square, turned, turned],
+        functools.partial(
+            early_kernel, [held[name][0] for name in EARLY], late_places
+        ),
+        out_shape=[
+            square,
+            square,
+            turned,
+            turned,
+            jax.ShapeDtypeStruct((-(-count // BITS), 128), jnp.int32),
+        ],
         in_specs=[SMEM] + [VMEM] * (len(EARLY) + 4),
-        out_specs=[VMEM] * 4,
+        out_specs=[VMEM] * 5,
         compiler_params=params(24 if n > 16 else 8),
         name="early",
     )(coupling, mine_z, other_z, other_own, block, *[held[name][1] for name in EARLY])
     mine, other, send, keep = pl.pallas_call(
-        functools.partial(product_kernel, n, [held[name][0] for name in late]),
+        functools.partial(product_kernel, n, late_places),
         out_shape=[square, square]
         + [jax.ShapeDtypeStruct((NCH * CW // 2, CW), jnp.float32)] * 2,
-        in_specs=[SMEM] + [VMEM] * (len(late) + 6),
+        in_specs=[VMEM] * (len(late) + 7),
         out_specs=[VMEM] * 4,
         compiler_params=params(24 if n > 16 else 8),
         name="product",
-    )(
-        coupling,
-        mine_z,
-        other_z,
-        *partial,
-        *[held[name][1] for name in late],
-    )
+    )(mine_z, other_z, *partial, *[held[name][1] for name in late])
     got = exchange(send, n, (1, 1))
     piece = NCH * CW // n
     width = NCH * CW // 2 // len(QUAD)

time: 38.5 us -> 37.4 us (0.971)
  Pallas kernels: 8.05 us -> 6.79 us
  starting transfers between devices: 17.8 us -> 18.4 us
  waiting for transfers between devices: 11.6 us -> 11.2 us
    pallas_call x1, Pallas kernels: 1.79 us -> 0.89 us  [per_device(): pl.pallas_call(functools.partial(early_kernel, [held[name][0] for name in...]
    ppermute x14, starting transfers between devices: 17.8 us -> 18.4 us  [exchange(): return lax.ppermute(block, 'row', [(i, i ^ masks[i % 2]) for i in range(n)])]
  transfers between devices with their start and end apart: 14 -> 14, of which waited for: 9 -> 9; matrix products, arithmetic and copies ran while one was open for 0% -> 0% of each run, Pallas kernels for 13% -> 11%
where the time goes in v5:
time: 37.4 us; the launch traced here: 37.1 us
  starting transfers between devices  18.4 us (49%)
  waiting for transfers between devices  11.2 us (30%)
  Pallas kernels  6.79 us (18%)
  between operations  0.71 us (2%)
    ppermute x14, starting transfers between devices, exchange(): return lax.ppermute(block, 'row', [(i, i ^ masks[i % 2]) for i in range(n)])  18.4 us
    ppermute x14, waiting for transfers between devices, exchange(): return lax.ppermute(block, 'row', [(i, i ^ masks[i % 2]) for i in range(n)])  11.2 us
    pallas_call x1, Pallas kernels, gather(): pl.pallas_call(load_kernel, out_shape=[half, half], in_specs=[ANY, ANY],...  1.76 us
    pallas_call x1, Pallas kernels, per_device(): pl.pallas_call(offdiag_kernel, out_shape=[jax.ShapeDtypeStruct((rows, NCH...  1.39 us
    pallas_call x1, Pallas kernels, per_device(): pl.pallas_call(functools.partial(product_kernel, n, late_places), out_sha...  1.07 us
    pallas_call x1, Pallas kernels, per_device(): pl.pallas_call(compact_kernel, out_shape=pltpu.VMEM((rows, CW), lower_pan...  0.98 us
    pallas_call x1, Pallas kernels, per_device(): pl.pallas_call(functools.partial(early_kernel, [held[name][0] for name in...  0.89 us
  transfers between devices with their start and end apart: 14, of which 9 were waited for; matrix products, arithmetic and copies ran while one was open for 0% of the time, Pallas kernels for 11%

profile of v5, /device:TPU:0, one launch (start us, length us, event | category | flops | bytes accessed | tf_op | source)
XLA Modules:
  0.0 37.1 jit_solution(5676149692031708711)
XLA Ops:
  0.6 1.0 %compact.1.own_ref.refs_0_.low_ref = bf16[256,256]{1,0:T(8,128)(2,1)S(1)} custom-call(s32[16]{0:T(128)} %coupling_ref.5, bf16[256,512]{1,0:T(8,128)(2,1)} %panel_ref.1), custom_call_target="tpu_custom_call" | custom-call | tf_op jit(solution)/shard_map/compact/pallas_call | solution.py:238
  1.6 0.5 %collective-permute-start = (bf16[256,4096]{1,0:T(8,128)(2,1)}, bf16[256,4096]{1,0:T(8,128)(2,1)S(1)}, u32[]{:S(2)}, u32[]{:S(2)}) collective-permute-start(bf16[256,4096]{1,0:T(8,128)(2,1)} %mine_hbm.1), channel_id=1, source_target_pairs={{0,1},{1,0},{2,3},{3,2},{4,5},{5,4},{6,7},{7,6},{8,9},{9,8},{10,11... | collective-permute-start | bytes 6291464 | tf_op jit(solution)/shard_map/ppermute | solution.py:28
  2.1 2.6 %collective-permute-start.2 = (bf16[256,256]{1,0:T(8,128)(2,1)S(1)}, bf16[256,256]{1,0:T(8,128)(2,1)S(1)}, u32[]{:S(2)}, u32[]{:S(2)}) collective-permute-start(bf16[256,256]{1,0:T(8,128)(2,1)S(1)} %compact.1.own_ref.refs_0_.low_ref), channel_id=1, source_target_pairs={{0,2},{1,5},{2,0},{3,7},{4,6},{5,1},{6,4},{7,3},{8,10},{9,13},{10,... | collective-permute-start | bytes 393224 | tf_op jit(solution)/shard_map/ppermute | solution.py:28
  4.7 2.6 %collective-permute-start.3 = (bf16[256,256]{1,0:T(8,128)(2,1)S(1)}, bf16[256,256]{1,0:T(8,128)(2,1)S(1)}, u32[]{:S(2)}, u32[]{:S(2)}) collective-permute-start(bf16[256,256]{1,0:T(8,128)(2,1)S(1)} %compact.1.own_ref.refs_0_.low_ref), channel_id=1, source_target_pairs={{0,8},{1,9},{2,10},{3,11},{4,12},{5,13},{6,14},{7,15},{8,0},{9,1},... | collective-permute-start | bytes 393224 | tf_op jit(solution)/shard_map/ppermute | solution.py:28
  7.3 0.4 collective-permute-done.2.refs_1_.high_ref
  7.7 0.0 copy-start.1
  7.7 2.1 %collective-permute-start.4 = (bf16[512,256]{1,0:T(8,128)(2,1)S(1)}, bf16[512,256]{1,0:T(8,128)(2,1)S(1)}, u32[]{:S(2)}, u32[]{:S(2)}) collective-permute-start(bf16[512,256]{1,0:T(8,128)(2,1)S(1)} %join.1), channel_id=1, source_target_pairs={{0,4},{1,3},{2,6},{3,1},{4,0},{5,7},{6,2},{7,5},{8,12},{9,11},{10,... | collective-permute-start | bytes 786440 | tf_op jit(solution)/shard_map/ppermute | solution.py:28
  9.9 0.0 collective-permute-start.1
  9.9 4.3 %collective-permute-done.3.refs_2_ = bf16[256,256]{1,0:T(8,128)(2,1)S(1)} collective-permute-done((bf16[256,256]{1,0:T(8,128)(2,1)S(1)}, bf16[256,256]{1,0:T(8,128)(2,1)S(1)}, u32[]{:S(2)}, u32[]{:S(2)}) %collective-permute-start.3) | collective-permute-done | bytes 131104 | tf_op jit(solution)/shard_map/ppermute | solution.py:28
  14.2 0.5 %collective-permute-start.5 = (bf16[256,256]{1,0:T(8,128)(2,1)S(1)}, bf16[256,256]{1,0:T(8,128)(2,1)S(1)}, u32[]{:S(2)}, u32[]{:S(2)}) collective-permute-start(bf16[256,256]{1,0:T(8,128)(2,1)S(1)} %collective-permute-done.3.refs_2_), channel_id=1, source_target_pairs={{0,6},{1,7},{2,4},{3,5},{4,2},{5,3},{6,0},{7,1},{8,14},{9,15},{10,... | collective-permute-start | bytes 393224 | tf_op jit(solution)/shard_map/ppermute | solution.py:28
  14.7 0.6 %collective-permute-start.6 = (bf16[256,256]{1,0:T(8,128)(2,1)S(1)}, bf16[256,256]{1,0:T(8,128)(2,1)S(1)}, u32[]{:S(2)}, u32[]{:S(2)}) collective-permute-start(bf16[256,256]{1,0:T(8,128)(2,1)S(1)} %collective-permute-done.3.refs_2_), channel_id=1, source_target_pairs={{0,2},{1,5},{2,0},{3,7},{4,6},{5,1},{6,4},{7,3},{8,10},{9,13},{10,... | collective-permute-start | bytes 393224 | tf_op jit(solution)/shard_map/ppermute | solution.py:28
  15.2 0.0 collective-permute-done.other_hbm
  15.2 0.0 copy-start.2
  15.2 2.4 %collective-permute-start.7 = (bf16[256,256]{1,0:T(8,128)(2,1)S(1)}, bf16[256,256]{1,0:T(8,128)(2,1)S(1)}, u32[]{:S(2)}, u32[]{:S(2)}) collective-permute-start(bf16[256,256]{1,0:T(8,128)(2,1)S(1)} %collective-permute-done.3.refs_2_), channel_id=1, source_target_pairs={{0,4},{1,3},{2,6},{3,1},{4,0},{5,7},{6,2},{7,5},{8,12},{9,11},{10,... | collective-permute-start | bytes 393224 | tf_op jit(solution)/shard_map/ppermute | solution.py:28
  17.7 0.0 copy-done.2
  17.7 1.8 %load.1 = (bf16[256,2048]{1,0:T(8,128)(2,1)S(1)}, bf16[256,2048]{1,0:T(8,128)(2,1)S(1)}) custom-call(bf16[256,4096]{1,0:T(8,128)(2,1)} %mine_hbm.1, bf16[256,4096]{1,0:T(8,128)(2,1)} %copy-done.2), custom_call_target="tpu_custom_call" | custom-call | tf_op jit(solution)/shard_map/load/pallas_call | solution.py:207
  19.4 0.0 collective-permute-done.1.other_own
  19.4 0.0 copy-done.1
  19.4 0.9 %early.1 = (f32[256,256]{1,0:T(8,128)S(1)}, f32[256,256]{1,0:T(8,128)S(1)}, bf16[256,256]{1,0:T(8,128)(2,1)S(1)}, bf16[256,256]{1,0:T(8,128)(2,1)S(1)}, s32[1,128]{1,0:T(1,128)S(1)}) custom-call(s32[16]{0:T(128)S(1)} %copy-done.1, bf16[256,2048]{1,0:T(8,128)(2,1)S(1)} %get-tuple-element.23.mine_z, bf16[256,2048]{1,0:T(8,128)(2,1)S(1)} %get-tuple-element.24.other_z, ...), custom_call_target="tpu_custom_call" | custom-call | tf_op jit(solution)/shard_map/early/pallas_call | solution.py:252
  20.3 0.8 %collective-permute-done.5.refs_6_ = bf16[256,256]{1,0:T(8,128)(2,1)S(1)} collective-permute-done((bf16[256,256]{1,0:T(8,128)(2,1)S(1)}, bf16[256,256]{1,0:T(8,128)(2,1)S(1)}, u32[]{:S(2)}, u32[]{:S(2)}) %collective-permute-start.5) | collective-permute-done | bytes 131104 | tf_op jit(solution)/shard_map/ppermute | solution.py:28
  21.2 1.3 %collective-permute-done.6.refs_7_ = bf16[256,256]{1,0:T(8,128)(2,1)S(1)} collective-permute-done((bf16[256,256]{1,0:T(8,128)(2,1)S(1)}, bf16[256,256]{1,0:T(8,128)(2,1)S(1)}, u32[]{:S(2)}, u32[]{:S(2)}) %collective-permute-start.6) | collective-permute-done | bytes 131104 | tf_op jit(solution)/shard_map/ppermute | solution.py:28
  22.4 0.2 collective-permute-done.7.refs_8_
  22.6 0.0 collective-permute-done.4.refs_5_
  22.6 0.0 copy-start
  22.6 1.1 %product.1 = (f32[256,256]{1,0:T(8,128)S(1)}, f32[256,256]{1,0:T(8,128)S(1)}, f32[256,256]{1,0:T(8,128)S(1)}, f32[256,256]{1,0:T(8,128)S(1)}) custom-call(bf16[256,2048]{1,0:T(8,128)(2,1)S(1)} %get-tuple-element.23.mine_z, bf16[256,2048]{1,0:T(8,128)(2,1)S(1)} %get-tuple-element.24.other_z, f32[256,256]{1,0:T(8,128)S(1)} %get-tuple-element.25.refs_0_, ...), custom_call_target="tpu_custom_call" | custom-call | tf_op jit(solution)/shard_map/product/pallas_call | solution.py:268
  23.7 0.1 collective-permute-start.9
  23.8 0.5 %collective-permute-start.8 = (f32[256,256]{1,0:T(8,128)S(1)}, f32[256,256]{1,0:T(8,128)S(1)}, u32[]{:S(2)}, u32[]{:S(2)}) collective-permute-start(f32[256,256]{1,0:T(8,128)S(1)} %get-tuple-element.31), channel_id=1, source_target_pairs={{0,1},{1,0},{2,3},{3,2},{4,5},{5,4},{6,7},{7,6},{8,9},{9,8},{10,11... | collective-permute-start | bytes 786440 | tf_op jit(solution)/shard_map/ppermute | solution.py:28
  24.3 1.0 %collective-permute-done.9.got_ref = f32[256,256]{1,0:T(8,128)S(1)} collective-permute-done((f32[256,256]{1,0:T(8,128)S(1)}, f32[256,256]{1,0:T(8,128)S(1)}, u32[]{:S(2)}, u32[]{:S(2)}) %collective-permute-start.9) | collective-permute-done | bytes 262176 | tf_op jit(solution)/shard_map/ppermute | solution.py:28
  25.3 0.1 collective-permute-start.10
  25.5 1.6 %collective-permute-start.11 = (f32[64,256]{1,0:T(8,128)S(1)}, f32[64,256]{1,0:T(8,128)S(1)}, u32[]{:S(2)}, u32[]{:S(2)}) collective-permute-start(f32[64,256]{1,0:T(8,128)S(1)} %get-tuple-element.37), channel_id=1, source_target_pairs={{0,2},{1,5},{2,0},{3,7},{4,6},{5,1},{6,4},{7,3},{8,10},{9,13},{10,... | collective-permute-start | bytes 196616 | tf_op jit(solution)/shard_map/ppermute | solution.py:28
  27.1 1.8 %collective-permute-start.12 = (f32[64,256]{1,0:T(8,128)S(1)}, f32[64,256]{1,0:T(8,128)S(1)}, u32[]{:S(2)}, u32[]{:S(2)}) collective-permute-start(f32[64,256]{1,0:T(8,128)S(1)} %get-tuple-element.38), channel_id=1, source_target_pairs={{0,4},{1,3},{2,6},{3,1},{4,0},{5,7},{6,2},{7,5},{8,12},{9,11},{10,... | collective-permute-start | bytes 196616 | tf_op jit(solution)/shard_map/ppermute | solution.py:28
  28.9 2.3 %collective-permute-done.10.refs_1_ = f32[64,256]{1,0:T(8,128)S(1)} collective-permute-done((f32[64,256]{1,0:T(8,128)S(1)}, f32[64,256]{1,0:T(8,128)S(1)}, u32[]{:S(2)}, u32[]{:S(2)}) %collective-permute-start.10) | collective-permute-done | bytes 65568 | tf_op jit(solution)/shard_map/ppermute | solution.py:28
  31.1 0.5 %collective-permute-done.11.refs_2_ = f32[64,256]{1,0:T(8,128)S(1)} collective-permute-done((f32[64,256]{1,0:T(8,128)S(1)}, f32[64,256]{1,0:T(8,128)S(1)}, u32[]{:S(2)}, u32[]{:S(2)}) %collective-permute-start.11) | collective-permute-done | bytes 65568 | tf_op jit(solution)/shard_map/ppermute | solution.py:28
  31.6 0.0 collective-permute-done.12.refs_3_
  31.6 2.9 %collective-permute-start.13 = (f32[32,256]{1,0:T(8,128)S(1)}, f32[32,256]{1,0:T(8,128)S(1)}, u32[]{:S(2)}, u32[]{:S(2)}) collective-permute-start(f32[32,256]{1,0:T(8,128)S(1)} %get-tuple-element.40), channel_id=1, source_target_pairs={{0,8},{1,9},{2,10},{3,11},{4,12},{5,13},{6,14},{7,15},{8,0},{9,1},... | collective-permute-start | bytes 98312 | tf_op jit(solution)/shard_map/ppermute | solution.py:28
  34.5 0.0 collective-permute-done.8.other_ref
  34.5 1.4 %offdiag.1 = (f32[256,512]{1,0:T(8,128)}, f32[8,128]{1,0:T(8,128)S(1)}) custom-call(s32[16]{0:T(128)S(1)} %copy-done.1, f32[256,256]{1,0:T(8,128)S(1)} %get-tuple-element.30.mine_ref, f32[256,256]{1,0:T(8,128)S(1)} %collective-permute-done.8.other_ref), custom_call_target="tpu_custom_call" | custom-call | tf_op jit(solution)/shard_map/offdiag/pallas_call | solution.py:302
  35.9 0.6 %collective-permute-done.13.got_ref = f32[32,256]{1,0:T(8,128)S(1)} collective-permute-done((f32[32,256]{1,0:T(8,128)S(1)}, f32[32,256]{1,0:T(8,128)S(1)}, u32[]{:S(2)}, u32[]{:S(2)}) %collective-permute-start.13) | collective-permute-done | bytes 32800 | tf_op jit(solution)/shard_map/ppermute | solution.py:28
  36.5 0.0 copy-done
  36.5 0.6 %last.1 = f32[32,256]{1,0:T(8,128)} custom-call(f32[32,256]{1,0:T(8,128)S(1)} %copy-done, f32[32,256]{1,0:T(8,128)S(1)} %get-tuple-element.39.kept_ref, f32[32,256]{1,0:T(8,128)S(1)} %collective-permute-done.13.got_ref, f32[8,128]{1,0:T(8,128)S(1)} %get-tuple-element.41.after_ref), custom_call_target="tpu_custom_call" | custom-call | tf_op jit(solution)/shard_map/last/pallas_call | solution.py:310
  (3 shorter events, 0.1 us)
Async XLA Ops:
  1.6 13.6 %collective-permute-start = (bf16[256,4096]{1,0:T(8,128)(2,1)}, bf16[256,4096]{1,0:T(8,128)(2,1)S(1)}, u32[]{:S(2)}, u32[]{:S(2)}) collective-permute-start(bf16[256,4096]{1,0:T(8,128)(2,1)} %mine_hbm.1), channel_id=1, source_target_pairs={{0,1},{1,0},{2,3},{3,2},{4,5},{5,4},{6,7},{7,6},{8,9},{9,8},{10,11... | collective-permute-start | bytes 6291464 | tf_op jit(solution)/shard_map/ppermute | solution.py:28
  2.1 5.5 %collective-permute-start.2 = (bf16[256,256]{1,0:T(8,128)(2,1)S(1)}, bf16[256,256]{1,0:T(8,128)(2,1)S(1)}, u32[]{:S(2)}, u32[]{:S(2)}) collective-permute-start(bf16[256,256]{1,0:T(8,128)(2,1)S(1)} %compact.1.own_ref.refs_0_.low_ref), channel_id=1, source_target_pairs={{0,2},{1,5},{2,0},{3,7},{4,6},{5,1},{6,4},{7,3},{8,10},{9,13},{10,... | collective-permute-start | bytes 393224 | tf_op jit(solution)/shard_map/ppermute | solution.py:28
  4.7 9.4 %collective-permute-start.3 = (bf16[256,256]{1,0:T(8,128)(2,1)S(1)}, bf16[256,256]{1,0:T(8,128)(2,1)S(1)}, u32[]{:S(2)}, u32[]{:S(2)}) collective-permute-start(bf16[256,256]{1,0:T(8,128)(2,1)S(1)} %compact.1.own_ref.refs_0_.low_ref), channel_id=1, source_target_pairs={{0,8},{1,9},{2,10},{3,11},{4,12},{5,13},{6,14},{7,15},{8,0},{9,1},... | collective-permute-start | bytes 393224 | tf_op jit(solution)/shard_map/ppermute | solution.py:28
  7.7 11.7 %copy-start.1 = (s32[16]{0:T(128)S(1)}, s32[16]{0:T(128)}, u32[]{:S(2)}) copy-start(s32[16]{0:T(128)} %coupling_ref.5) | copy-start | bytes 196
  7.7 14.9 %collective-permute-start.4 = (bf16[512,256]{1,0:T(8,128)(2,1)S(1)}, bf16[512,256]{1,0:T(8,128)(2,1)S(1)}, u32[]{:S(2)}, u32[]{:S(2)}) collective-permute-start(bf16[512,256]{1,0:T(8,128)(2,1)S(1)} %join.1), channel_id=1, source_target_pairs={{0,4},{1,3},{2,6},{3,1},{4,0},{5,7},{6,2},{7,5},{8,12},{9,11},{10,... | collective-permute-start | bytes 786440 | tf_op jit(solution)/shard_map/ppermute | solution.py:28
  9.9 9.6 %collective-permute-start.1 = (bf16[256,256]{1,0:T(8,128)(2,1)S(1)}, bf16[256,256]{1,0:T(8,128)(2,1)S(1)}, u32[]{:S(2)}, u32[]{:S(2)}) collective-permute-start(bf16[256,256]{1,0:T(8,128)(2,1)S(1)} %compact.1.own_ref.refs_0_.low_ref), channel_id=1, source_target_pairs={{0,1},{1,0},{2,3},{3,2},{4,5},{5,4},{6,7},{7,6},{8,9},{9,8},{10,11... | collective-permute-start | bytes 393224 | tf_op jit(solution)/shard_map/ppermute | solution.py:28
  14.2 7.0 %collective-permute-start.5 = (bf16[256,256]{1,0:T(8,128)(2,1)S(1)}, bf16[256,256]{1,0:T(8,128)(2,1)S(1)}, u32[]{:S(2)}, u32[]{:S(2)}) collective-permute-start(bf16[256,256]{1,0:T(8,128)(2,1)S(1)} %collective-permute-done.3.refs_2_), channel_id=1, source_target_pairs={{0,6},{1,7},{2,4},{3,5},{4,2},{5,3},{6,0},{7,1},{8,14},{9,15},{10,... | collective-permute-start | bytes 393224 | tf_op jit(solution)/shard_map/ppermute | solution.py:28
  14.7 7.8 %collective-permute-start.6 = (bf16[256,256]{1,0:T(8,128)(2,1)S(1)}, bf16[256,256]{1,0:T(8,128)(2,1)S(1)}, u32[]{:S(2)}, u32[]{:S(2)}) collective-permute-start(bf16[256,256]{1,0:T(8,128)(2,1)S(1)} %collective-permute-done.3.refs_2_), channel_id=1, source_target_pairs={{0,2},{1,5},{2,0},{3,7},{4,6},{5,1},{6,4},{7,3},{8,10},{9,13},{10,... | collective-permute-start | bytes 393224 | tf_op jit(solution)/shard_map/ppermute | solution.py:28
  15.2 2.4 %copy-start.2 = (bf16[256,4096]{1,0:T(8,128)(2,1)}, bf16[256,4096]{1,0:T(8,128)(2,1)S(1)}, u32[]{:S(2)}) copy-start(bf16[256,4096]{1,0:T(8,128)(2,1)S(1)} %collective-permute-done.other_hbm) | copy-start | bytes 6291460
  15.2 7.4 %collective-permute-start.7 = (bf16[256,256]{1,0:T(8,128)(2,1)S(1)}, bf16[256,256]{1,0:T(8,128)(2,1)S(1)}, u32[]{:S(2)}, u32[]{:S(2)}) collective-permute-start(bf16[256,256]{1,0:T(8,128)(2,1)S(1)} %collective-permute-done.3.refs_2_), channel_id=1, source_target_pairs={{0,4},{1,3},{2,6},{3,1},{4,0},{5,7},{6,2},{7,5},{8,12},{9,11},{10,... | collective-permute-start | bytes 393224 | tf_op jit(solution)/shard_map/ppermute | solution.py:28
  22.6 13.9 %copy-start = (f32[32,256]{1,0:T(8,128)S(1)}, f32[32,256]{1,0:T(8,128)}, u32[]{:S(2)}) copy-start(f32[32,256]{1,0:T(8,128)} %inverse_ref.1) | copy-start | bytes 98308
  23.7 1.6 %collective-permute-start.9 = (f32[256,256]{1,0:T(8,128)S(1)}, f32[256,256]{1,0:T(8,128)S(1)}, u32[]{:S(2)}, u32[]{:S(2)}) collective-permute-start(f32[256,256]{1,0:T(8,128)S(1)} %get-tuple-element.34), channel_id=1, source_target_pairs={{0,1},{1,0},{2,3},{3,2},{4,5},{5,4},{6,7},{7,6},{8,9},{9,8},{10,11... | collective-permute-start | bytes 786440 | tf_op jit(solution)/shard_map/ppermute | solution.py:28
  23.8 10.7 %collective-permute-start.8 = (f32[256,256]{1,0:T(8,128)S(1)}, f32[256,256]{1,0:T(8,128)S(1)}, u32[]{:S(2)}, u32[]{:S(2)}) collective-permute-start(f32[256,256]{1,0:T(8,128)S(1)} %get-tuple-element.31), channel_id=1, source_target_pairs={{0,1},{1,0},{2,3},{3,2},{4,5},{5,4},{6,7},{7,6},{8,9},{9,8},{10,11... | collective-permute-start | bytes 786440 | tf_op jit(solution)/shard_map/ppermute | solution.py:28
  25.3 5.8 %collective-permute-start.10 = (f32[64,256]{1,0:T(8,128)S(1)}, f32[64,256]{1,0:T(8,128)S(1)}, u32[]{:S(2)}, u32[]{:S(2)}) collective-permute-start(f32[64,256]{1,0:T(8,128)S(1)} %get-tuple-element.36), channel_id=1, source_target_pairs={{0,6},{1,7},{2,4},{3,5},{4,2},{5,3},{6,0},{7,1},{8,14},{9,15},{10,... | collective-permute-start | bytes 196616 | tf_op jit(solution)/shard_map/ppermute | solution.py:28
  25.5 6.1 %collective-permute-start.11 = (f32[64,256]{1,0:T(8,128)S(1)}, f32[64,256]{1,0:T(8,128)S(1)}, u32[]{:S(2)}, u32[]{:S(2)}) collective-permute-start(f32[64,256]{1,0:T(8,128)S(1)} %get-tuple-element.37), channel_id=1, source_target_pairs={{0,2},{1,5},{2,0},{3,7},{4,6},{5,1},{6,4},{7,3},{8,10},{9,13},{10,... | collective-permute-start | bytes 196616 | tf_op jit(solution)/shard_map/ppermute | solution.py:28
  27.1 4.5 %collective-permute-start.12 = (f32[64,256]{1,0:T(8,128)S(1)}, f32[64,256]{1,0:T(8,128)S(1)}, u32[]{:S(2)}, u32[]{:S(2)}) collective-permute-start(f32[64,256]{1,0:T(8,128)S(1)} %get-tuple-element.38), channel_id=1, source_target_pairs={{0,4},{1,3},{2,6},{3,1},{4,0},{5,7},{6,2},{7,5},{8,12},{9,11},{10,... | collective-permute-start | bytes 196616 | tf_op jit(solution)/shard_map/ppermute | solution.py:28
  31.6 4.9 %collective-permute-start.13 = (f32[32,256]{1,0:T(8,128)S(1)}, f32[32,256]{1,0:T(8,128)S(1)}, u32[]{:S(2)}, u32[]{:S(2)}) collective-permute-start(f32[32,256]{1,0:T(8,128)S(1)} %get-tuple-element.40), channel_id=1, source_target_pairs={{0,8},{1,9},{2,10},{3,11},{4,12},{5,13},{6,14},{7,15},{8,0},{9,1},... | collective-permute-start | bytes 98312 | tf_op jit(solution)/shard_map/ppermute | solution.py:28
